TPU v7x, 32 devices: a whole 2x2x4 slice. The times are simulated.
32 devices in a mesh: fsdp: 16 (over z, x, core), seq: 2 (over y).
Axes of the slice: x: 2, y: 2, z: 4, core: 2. Of those that a mesh axis runs over, the one named last changes fastest.
Arguments:
- latents: bfloat16 [16, 1024, 1024], P('fsdp', 'seq'), may hold values from -6 to 6
- conditioning: bfloat16 [16, 1024], P('fsdp'), may hold values from -6 to 6
- mod_weight: bfloat16 [1024, 6144], P('fsdp'), may hold values from -0.1875 to 0.1875
- mod_bias: bfloat16 [6144], P('fsdp'), may hold values from -2 to 2
- qkv_weight: bfloat16 [1024, 3072], P('fsdp'), may hold values from -0.1875 to 0.1875
- query_bias: bfloat16 [1024], P('fsdp'), may hold values from -3 to 3
- value_bias: bfloat16 [1024], P('fsdp'), may hold values from -3 to 3
- out_weight: bfloat16 [1024, 1024], P('fsdp'), may hold values from -3 to 3
- out_bias: bfloat16 [1024], P('fsdp'), may hold values from -2 to 2
- up_weight: bfloat16 [1024, 4096], P('fsdp'), may hold values from -0.1875 to 0.1875
- up_bias: bfloat16 [4096], P('fsdp'), may hold values from -3 to 3
- down_weight: bfloat16 [4096, 1024], P('fsdp'), may hold values from -0.09375 to 0.09375
- down_bias: bfloat16 [1024], P('fsdp'), may hold values from -2 to 2
- cotangent: bfloat16 [16, 1024, 1024], P('fsdp', 'seq'), may hold values from -6 to 6
Outputs:
- block_output: bfloat16 [16, 1024, 1024], P('fsdp', 'seq')
- latents_grad: float32 [16, 1024, 1024], P('fsdp', 'seq')
- conditioning_grad: float32 [16, 1024], P('fsdp')
- mod_weight_grad: float32 [1024, 6144], P('fsdp')
- mod_bias_grad: float32 [6144], P('fsdp')
- qkv_weight_grad: float32 [1024, 3072], P('fsdp')
- query_bias_grad: float32 [1024], P('fsdp')
- value_bias_grad: float32 [1024], P('fsdp')
- out_weight_grad: float32 [1024, 1024], P('fsdp')
- out_bias_grad: float32 [1024], P('fsdp')
- up_weight_grad: float32 [1024, 4096], P('fsdp')
- up_bias_grad: float32 [4096], P('fsdp')
- down_weight_grad: float32 [4096, 1024], P('fsdp')
- down_bias_grad: float32 [1024], P('fsdp')
All inputs are finite; a program needn't handle non-finite values.
Results may differ from a plain program's by a relative error of at most 0.01.
The roundings to bfloat16 on the way count: a program that leaves them out, or rounds other values in their place, can miss the bound.
Values may be sent and summed in bfloat16 or wider, within the bound.
A program may use at most 192 MiB of HBM per device.

v0:
```python
import math

import jax
import jax.numpy as jnp
from jax import lax
from jax.sharding import PartitionSpec as P

HD = 64


EPSILON = 1e-06


def norm_rows(values):
    centred = values - jnp.mean(values, axis=-1, keepdims=True)
    inverse = lax.rsqrt(jnp.mean(centred * centred, axis=-1, keepdims=True) + EPSILON)
    return (centred * inverse, inverse)


def norm_back(grad_normed, normed, inverse):
    mean_grad = jnp.mean(grad_normed, axis=-1, keepdims=True)
    mean_cross = jnp.mean(grad_normed * normed, axis=-1, keepdims=True)
    return inverse * (grad_normed - mean_grad - normed * mean_cross)


def project(left, weight):
    return lax.dot_general(
        left, weight, (((left.ndim - 1,), (0,)), ((), ())), preferred_element_type=jnp.float32
    )


def project_back(left, weight):
    return lax.dot_general(
        left, weight, (((left.ndim - 1,), (1,)), ((), ())), preferred_element_type=jnp.float32
    )


def weight_term(inputs, grads):
    return lax.dot_general(
        inputs, grads, (((0,), (0,)), ((), ())), preferred_element_type=jnp.float32
    )


def attend_forward(queries, keys, values, block):
    length, heads, size = queries.shape
    factor = 1.0 / math.sqrt(size)

    def one_block(query_block):
        scores = (
            jnp.einsum("qhd,khd->hqk", query_block, keys, preferred_element_type=jnp.float32)
            * factor
        )
        peak_score = jnp.max(scores, axis=-1, keepdims=True)
        exponent = jnp.exp(scores - peak_score)
        totals = jnp.sum(exponent, axis=-1, keepdims=True)
        probs = (exponent / totals).astype(jnp.bfloat16)
        mixed = jnp.einsum("hqk,khd->qhd", probs, values, preferred_element_type=jnp.float32)
        return (mixed.astype(jnp.bfloat16), (peak_score + jnp.log(totals))[..., 0])

    mixed, logsum = lax.map(one_block, queries.reshape(length // block, block, heads, size))
    return (mixed.reshape(length, heads * size), logsum)


def attend_backward(queries, keys, values, logsum, grad_out, block):
    length, heads, size = queries.shape
    factor = 1.0 / math.sqrt(size)

    def one_block(carry, pieces):
        key_grad, value_grad = carry
        query_block, grad_block, lse_block = pieces
        scores = (
            jnp.einsum("qhd,khd->hqk", query_block, keys, preferred_element_type=jnp.float32)
            * factor
        )
        probs = jnp.exp(scores - lse_block[..., None])
        value_grad = value_grad + jnp.einsum(
            "hqk,qhd->khd",
            probs.astype(jnp.bfloat16),
            grad_block,
            preferred_element_type=jnp.float32,
        )
        grad_probs = jnp.einsum(
            "qhd,khd->hqk", grad_block, values, preferred_element_type=jnp.float32
        )
        inner = jnp.sum(probs * grad_probs, axis=-1, keepdims=True)
        grad_scores = (probs * (grad_probs - inner)).astype(jnp.bfloat16)
        query_grad = (
            jnp.einsum("hqk,khd->qhd", grad_scores, keys, preferred_element_type=jnp.float32)
            * factor
        )
        key_grad = (
            key_grad
            + jnp.einsum(
                "hqk,qhd->khd", grad_scores, query_block, preferred_element_type=jnp.float32
            )
            * factor
        )
        return ((key_grad, value_grad), query_grad)

    zeros = jnp.zeros(keys.shape, jnp.float32)
    count = length // block
    (key_grad, value_grad), query_grad = lax.scan(
        one_block,
        (zeros, zeros),
        (
            queries.reshape(count, block, heads, size),
            grad_out.reshape(count, block, heads, size),
            logsum,
        ),
    )
    return (query_grad.reshape(length, heads, size), key_grad, value_grad)


def per_device(
    latents,
    conditioning,
    mod_weight,
    mod_bias,
    qkv_weight,
    query_bias,
    value_bias,
    out_weight,
    out_bias,
    up_weight,
    up_bias,
    down_weight,
    down_bias,
    cotangent,
):
    latent_count, local_len, width = latents.shape
    rows = latent_count * local_len
    (
        full_mod,
        full_mod_bias,
        full_qkv,
        full_query_bias,
        full_value_bias,
        full_out,
        full_out_bias,
        full_up,
        full_up_bias,
        full_down,
        full_down_bias,
    ) = (
        lax.all_gather(mod_weight, "fsdp", axis=0, tiled=True),
        lax.all_gather(mod_bias, "fsdp", axis=0, tiled=True),
        lax.all_gather(qkv_weight, "fsdp", axis=0, tiled=True),
        lax.all_gather(query_bias, "fsdp", axis=0, tiled=True),
        lax.all_gather(value_bias, "fsdp", axis=0, tiled=True),
        lax.all_gather(out_weight, "fsdp", axis=0, tiled=True),
        lax.all_gather(out_bias, "fsdp", axis=0, tiled=True),
        lax.all_gather(up_weight, "fsdp", axis=0, tiled=True),
        lax.all_gather(up_bias, "fsdp", axis=0, tiled=True),
        lax.all_gather(down_weight, "fsdp", axis=0, tiled=True),
        lax.all_gather(down_bias, "fsdp", axis=0, tiled=True),
    )
    cond_float = conditioning.astype(jnp.float32)
    silu_cond = jax.nn.silu(cond_float).astype(jnp.bfloat16)
    modulation = (project(silu_cond, full_mod) + full_mod_bias.astype(jnp.float32)).reshape(
        latent_count, 6, 1, width
    )
    shift_one = modulation[:, 0]
    scale_one = modulation[:, 1]
    gate_one = modulation[:, 2]
    shift_two = modulation[:, 3]
    scale_two = modulation[:, 4]
    gate_two = modulation[:, 5]
    inputs = latents.astype(jnp.float32)
    normed_one, inverse_one = norm_rows(inputs)
    attn_input = (normed_one * (1.0 + scale_one) + shift_one).astype(jnp.bfloat16)
    bias_all = jnp.concatenate(
        [full_query_bias, jnp.zeros_like(full_query_bias), full_value_bias]
    ).astype(jnp.float32)
    projected = (
        (project(attn_input, full_qkv) + bias_all)
        .astype(jnp.bfloat16)
        .reshape(latent_count, local_len, 3, width)
    )
    by_heads = lax.all_to_all(projected, "seq", split_axis=3, concat_axis=1, tiled=True)
    length = by_heads.shape[1]
    part = by_heads.shape[3]
    heads_local = part // HD
    block = min(512, length)

    def forward_latent(group):
        queries = group[:, 0].reshape(length, heads_local, HD)
        keys = group[:, 1].reshape(length, heads_local, HD)
        values = group[:, 2].reshape(length, heads_local, HD)
        return attend_forward(queries, keys, values, block)

    mixed, logsum = lax.map(forward_latent, by_heads)
    attn_heads = lax.all_to_all(mixed, "seq", split_axis=1, concat_axis=2, tiled=True)
    attn_out = project(attn_heads, full_out) + full_out_bias.astype(jnp.float32)
    after_attn = inputs + gate_one * attn_out
    normed_two, inverse_two = norm_rows(after_attn)
    mlp_input = (normed_two * (1.0 + scale_two) + shift_two).astype(jnp.bfloat16)
    hidden_pre = project(mlp_input, full_up) + full_up_bias.astype(jnp.float32)
    hidden_act, gelu_back = jax.vjp(lambda value: jax.nn.gelu(value, approximate=True), hidden_pre)
    hidden_act = hidden_act.astype(jnp.bfloat16)
    branch_out = project(hidden_act, full_down) + full_down_bias.astype(jnp.float32)
    block_output = (after_attn + gate_two * branch_out).astype(jnp.bfloat16)
    back_mod, back_qkv, back_out, back_up, back_down = (
        lax.all_gather(mod_weight, "fsdp", axis=0, tiled=True),
        lax.all_gather(qkv_weight, "fsdp", axis=0, tiled=True),
        lax.all_gather(out_weight, "fsdp", axis=0, tiled=True),
        lax.all_gather(up_weight, "fsdp", axis=0, tiled=True),
        lax.all_gather(down_weight, "fsdp", axis=0, tiled=True),
    )
    grad_out = cotangent.astype(jnp.float32)
    grad_branch = (gate_two * grad_out).astype(jnp.bfloat16)
    grad_gate_two = jnp.sum(grad_out * branch_out, axis=1)
    flat_branch = grad_branch.reshape(rows, width)
    down_term = weight_term(hidden_act.reshape(rows, -1), flat_branch)
    down_bias_term = jnp.sum(flat_branch.astype(jnp.float32), axis=0)
    grad_act = project_back(grad_branch, back_down)
    grad_pre = gelu_back(grad_act)[0].astype(jnp.bfloat16)
    flat_pre = grad_pre.reshape(rows, -1)
    up_term = weight_term(mlp_input.reshape(rows, width), flat_pre)
    up_bias_term = jnp.sum(flat_pre.astype(jnp.float32), axis=0)
    up_shard, up_bias_shard, down_shard, down_bias_shard = (
        lax.psum_scatter(up_term, "fsdp", scatter_dimension=0, tiled=True),
        lax.psum_scatter(up_bias_term, "fsdp", scatter_dimension=0, tiled=True),
        lax.psum_scatter(down_term, "fsdp", scatter_dimension=0, tiled=True),
        lax.psum_scatter(down_bias_term, "fsdp", scatter_dimension=0, tiled=True),
    )
    grad_mlp_in = project_back(grad_pre, back_up)
    grad_scale_two = jnp.sum(grad_mlp_in * normed_two, axis=1)
    grad_shift_two = jnp.sum(grad_mlp_in, axis=1)
    grad_after = grad_out + norm_back(grad_mlp_in * (1.0 + scale_two), normed_two, inverse_two)
    grad_attn = (gate_one * grad_after).astype(jnp.bfloat16)
    grad_gate_one = jnp.sum(grad_after * attn_out, axis=1)
    flat_attn = grad_attn.reshape(rows, width)
    out_term = weight_term(attn_heads.reshape(rows, width), flat_attn)
    out_bias_term = jnp.sum(flat_attn.astype(jnp.float32), axis=0)
    grad_heads_local = project_back(grad_attn, back_out).astype(jnp.bfloat16)
    grad_mixed = lax.all_to_all(grad_heads_local, "seq", split_axis=2, concat_axis=1, tiled=True)

    def backward_latent(pieces):
        group, lse_group, grad_group = pieces
        queries = group[:, 0].reshape(length, heads_local, HD)
        keys = group[:, 1].reshape(length, heads_local, HD)
        values = group[:, 2].reshape(length, heads_local, HD)
        query_grad, key_grad, value_grad = attend_backward(
            queries, keys, values, lse_group, grad_group.reshape(length, heads_local, HD), block
        )
        stacked = jnp.stack([query_grad, key_grad, value_grad], axis=1)
        return stacked.reshape(length, 3, part).astype(jnp.bfloat16)

    grad_by_heads = lax.map(backward_latent, (by_heads, logsum, grad_mixed))
    grad_projected = lax.all_to_all(
        grad_by_heads, "seq", split_axis=1, concat_axis=3, tiled=True
    ).reshape(latent_count, local_len, 3 * width)
    flat_projected = grad_projected.reshape(rows, 3 * width)
    qkv_term = weight_term(attn_input.reshape(rows, width), flat_projected)
    column_sums = jnp.sum(flat_projected.astype(jnp.float32), axis=0).reshape(3, width)
    query_bias_term = column_sums[0]
    value_bias_term = column_sums[2]
    grad_attn_in = project_back(grad_projected, back_qkv)
    grad_scale_one = jnp.sum(grad_attn_in * normed_one, axis=1)
    grad_shift_one = jnp.sum(grad_attn_in, axis=1)
    latents_grad = grad_after + norm_back(grad_attn_in * (1.0 + scale_one), normed_one, inverse_one)
    grad_mod_local = jnp.stack(
        [
            grad_shift_one,
            grad_scale_one,
            grad_gate_one,
            grad_shift_two,
            grad_scale_two,
            grad_gate_two,
        ],
        axis=1,
    ).reshape(latent_count, 6 * width)
    grad_modulation = lax.psum(grad_mod_local, "seq").astype(jnp.bfloat16)
    mod_term = weight_term(silu_cond, grad_modulation)
    mod_bias_term = jnp.sum(grad_modulation.astype(jnp.float32), axis=0)
    grad_silu = project_back(grad_modulation, back_mod)
    silu_value, silu_back = jax.vjp(jax.nn.silu, cond_float)
    conditioning_grad = silu_back(grad_silu)[0]
    (
        mod_shard,
        mod_bias_shard,
        qkv_shard,
        query_bias_shard,
        value_bias_shard,
        out_shard,
        out_bias_shard,
    ) = (
        lax.psum_scatter(mod_term, "fsdp", scatter_dimension=0, tiled=True),
        lax.psum_scatter(mod_bias_term, "fsdp", scatter_dimension=0, tiled=True),
        lax.psum_scatter(qkv_term, "fsdp", scatter_dimension=0, tiled=True),
        lax.psum_scatter(query_bias_term, "fsdp", scatter_dimension=0, tiled=True),
        lax.psum_scatter(value_bias_term, "fsdp", scatter_dimension=0, tiled=True),
        lax.psum_scatter(out_term, "fsdp", scatter_dimension=0, tiled=True),
        lax.psum_scatter(out_bias_term, "fsdp", scatter_dimension=0, tiled=True),
    )
    (
        qkv_total,
        query_bias_total,
        value_bias_total,
        out_total,
        out_bias_total,
        up_total,
        up_bias_total,
        down_total,
        down_bias_total,
    ) = lax.psum(
        (
            qkv_shard,
            query_bias_shard,
            value_bias_shard,
            out_shard,
            out_bias_shard,
            up_shard,
            up_bias_shard,
            down_shard,
            down_bias_shard,
        ),
        "seq",
    )
    return (
        block_output,
        latents_grad,
        conditioning_grad,
        mod_shard,
        mod_bias_shard,
        qkv_total,
        query_bias_total,
        value_bias_total,
        out_total,
        out_bias_total,
        up_total,
        up_bias_total,
        down_total,
        down_bias_total,
    )


def solution(mesh):
    return jax.shard_map(
        per_device,
        mesh=mesh,
        in_specs=(
            P("fsdp", "seq", None),
            P("fsdp", None),
            P("fsdp", None),
            P("fsdp"),
            P("fsdp", None),
            P("fsdp"),
            P("fsdp"),
            P("fsdp", None),
            P("fsdp"),
            P("fsdp", None),
            P("fsdp"),
            P("fsdp", None),
            P("fsdp"),
            P("fsdp", "seq", None),
        ),
        out_specs=(
            P("fsdp", "seq", None),
            P("fsdp", "seq", None),
            P("fsdp", None),
            P("fsdp", None),
            P("fsdp"),
            P("fsdp", None),
            P("fsdp"),
            P("fsdp"),
            P("fsdp", None),
            P("fsdp"),
            P("fsdp", None),
            P("fsdp"),
            P("fsdp", None),
            P("fsdp"),
        ),
        check_vma=False,
    )
```

profile of v0, /device:TPU:0, one launch (start us, length us, event | category | flops | bytes accessed | tf_op | source)
XLA Modules:
  0.0 1474.3 jit_solution(1265750515276939496)
XLA Ops:
  14.8 37.8 %all-reduce.13 = (bf16[1024]{0:T(1024)(128)(2,1)S(1)}, bf16[1024]{0:T(1024)(128)(2,1)S(1)}, bf16[1024]{0:T(1024)(128)(2,1)}, bf16[1024]{0:T(1024)(128)(2,1)}) all-reduce(bf16[1024]{0:T(1024)(128)(2,1)S(1)} %dynamic-update-slice.1, bf16[1024]{0:T(1024)(128)(2,1)S(1)} %dynamic-update-slice, ...), channel_id=1, replica_groups=mesh['fsdp'=16,'seq'=2] {'fsdp'}, use_global_device_ids=true, to_apply=%add.1 | all-reduce | flops 4096 | bytes 16384
  52.6 17.7 %all-gather = bf16[16,1,384]{2,1,0:T(2,128)(2,1)S(1)} all-gather(bf16[1,1,384]{2,1,0:T(2,128)(2,1)S(1)} %reshape.416), channel_id=1, replica_groups=mesh['fsdp'=16,'seq'=2] {'fsdp'}, dimensions={0}, use_global_device_ids=true | all-gather | bytes 13056 | tf_op jit(solution)/shard_map/all_gather | solution.py:146
  70.3 44.2 %all-gather.8.cloned.1.call-done = bf16[1024,6144]{1,0:T(8,128)(2,1)} async-done(((bf16[64,6144]{1,0:T(8,128)(2,1)}), bf16[1024,6144]{1,0:T(8,128)(2,1)}) %all-gather.8.cloned.1.call-update) | async-done | bytes 12582928 | tf_op jit(solution)/shard_map/all_gather | solution.py:145
  121.5 55.5 %all-gather.10.cloned.1.call-done = bf16[1024,3072]{1,0:T(8,128)(2,1)} async-done(((bf16[64,3072]{1,0:T(8,128)(2,1)}), bf16[1024,3072]{1,0:T(8,128)(2,1)}) %all-gather.10.cloned.1.call-update) | async-done | bytes 6291472 | tf_op jit(solution)/shard_map/all_gather | solution.py:147
  202.0 48.1 %all-to-all-done = bf16[1,512,3,1024]{1,2,0,3:T(4,128)(2,1)} async-done(((bf16[1,512,3,1024]{1,2,0,3:T(4,128)(2,1)}), bf16[1,512,3,1024]{1,2,0,3:T(4,128)(2,1)}, u32[]{:S(2)}, u32[]{:S(2)}) %all-to-all-start) | async-done | bytes 3145760 | tf_op jit(solution)/shard_map/all_to_all | solution.py:179
  271.5 21.9 %while.45 = (s32[]{:T(128)}, bf16[2,512,8,64]{1,3,2,0:T(8,128)(2,1)}, f32[2,8,512]{2,1,0:T(8,128)S(1)}, bf16[2,512,8,64]{1,3,2,0:T(8,128)(2,1)S(1)}, bf16[1024,8...) while((s32[]{:T(128)}, bf16[2,512,8,64]{1,3,2,0:T(8,128)(2,1)}, ...), condition=%wide.region_5.6_spmd, body=%wide.region_2.5_spmd.sunk | while | flops 1111748608 | bytes 57803376 | solution.py:60
  322.2 19.0 %all-gather.1 = bf16[16,1,256]{2,1,0:T(2,128)(2,1)S(1)} all-gather(bf16[1,1,256]{2,1,0:T(2,128)(2,1)S(1)} %reshape.418), channel_id=1, replica_groups=mesh['fsdp'=16,'seq'=2] {'fsdp'}, dimensions={0}, use_global_device_ids=true | all-gather | bytes 8704 | tf_op jit(solution)/shard_map/all_gather | solution.py:153
  356.1 11.9 fusion.88
  370.1 14.3 convert_reduce_fusion
  389.6 12.4 fusion.56
  451.1 88.6 %while.46 = (s32[]{:T(128)}, f32[1024,8,64]{0,2,1:T(8,128)}, f32[1024,8,64]{0,2,1:T(8,128)}, bf16[2,512,8,64]{1,3,2,0:T(8,128)(2,1)}, bf16[2,512,8,64]{1,3,2,0:T...) while((s32[]{:T(128)}, f32[1024,8,64]{0,2,1:T(8,128)}, ...), condition=%wide.region_12.13_spmd.clone, body=%wide.region_10.12_spmd.clone.sunk | while | flops 2737565696 | bytes 274843328 | solution.py:102
  453.5 11.1 multiply_reduce_fusion.8
  497.6 10.8 multiply_reduce_fusion.8
  555.3 51.4 %all_to_all.60 = bf16[1,1024,3,512]{3,2,0,1:T(4,128)(2,1)S(1)} all-to-all(bf16[1,1024,3,512]{3,2,0,1:T(4,128)(2,1)} %copy.92), channel_id=1, replica_groups=mesh['fsdp'=16,'seq'=2] {'seq'}, dimensions={1} | all-to-all | bytes 6291456 | tf_op jit(solution)/shard_map/all_to_all | solution.py:250
  624.4 13.1 fusion.86
  638.9 17.9 %fusion.67 = f32[4096,1024]{1,0:T(8,128)} fusion(bf16[1,512,1024]{2,1,0:T(8,128)(2,1)S(1)} %copy-done.14, f32[1024]{0:T(1024)S(1)} %bitcast.256, f32[512,4096]{1,0:T(8,128)} %fusion.88, f32[4096]{0:T(1024)S(1)} %bitcast.266), kind=kOutput, calls=%fused_computation.103 | convolution fusion | flops 4317511680 | bytes 26234880 | tf_op jit(solution)/shard_map/dot_general | solution.py:39
  666.4 88.8 %reduce-scatter.8.cloned.1.call-done = f32[64,3072]{1,0:T(8,128)} async-done(((f32[1024,3072]{1,0:T(8,128)}), f32[64,3072]{1,0:T(8,128)}) %reduce-scatter.8.cloned.1.call-update) | async-done | bytes 786448 | tf_op jit(solution)/shard_map/reduce_scatter | solution.py:290
  755.2 182.5 %reduce-scatter.12.cloned.1.call-done = f32[64,4096]{1,0:T(8,128)} async-done(((f32[1024,4096]{1,0:T(8,128)}), f32[64,4096]{1,0:T(8,128)}) %reduce-scatter.12.cloned.1.call-update) | async-done | bytes 1048592 | tf_op jit(solution)/shard_map/reduce_scatter | solution.py:221
  937.7 182.2 %reduce-scatter.14.cloned.1.call-done = f32[256,1024]{1,0:T(8,128)} async-done(((f32[4096,1024]{1,0:T(8,128)}), f32[256,1024]{1,0:T(8,128)}) %reduce-scatter.14.cloned.1.call-update) | async-done | bytes 1048592 | tf_op jit(solution)/shard_map/reduce_scatter | solution.py:223
  1126.3 15.9 %psum.70 = bf16[1,6144]{1,0:T(2,128)(2,1)S(1)} all-reduce(f32[1,6144]{1,0:T(1,128)S(1)} %bitcast.243), channel_id=1, replica_groups=mesh['fsdp'=16,'seq'=2] {'seq'}, use_global_device_ids=true, to_apply=%region_21.22 | all-reduce | flops 6144 | bytes 36864 | tf_op jit(solution)/shard_map/psum | solution.py:273
  1142.3 11.6 broadcast_multiply_fusion
  1158.3 58.1 %all-reduce.10 = (f32[6144]{0:T(1024)S(1)}, f32[1024]{0:T(1024)S(1)}, f32[1024]{0:T(1024)S(1)}, f32[1024]{0:T(1024)S(1)}, f32[4096]{0:T(1024)S(1)}, /*index=5*/f32[1024]{0:T(1024)S(1)}) all-reduce(bf16[6144]{0:T(1024)(128)(2,1)S(1)} %convert_reduce_fusion.5, ...), channel_id=3, replica_groups=mesh['fsdp'=16,'seq'=2] {'fsdp'}, use_global_device_ids=true, to_apply=%region_23.24.clone | all-reduce | flops 14336 | bytes 102400
  1222.9 10.8 fusion.77
  1233.8 226.8 %reduce-scatter.6.cloned.1.call-done = f32[64,6144]{1,0:T(8,128)} async-done(((f32[1024,6144]{1,0:T(8,128)}), f32[64,6144]{1,0:T(8,128)}) %reduce-scatter.6.cloned.1.call-update) | async-done | bytes 1572880 | tf_op jit(solution)/shard_map/reduce_scatter | solution.py:288
  (274 shorter events, 314.9 us)
Async XLA Ops:
  7.3 107.3 %copy-start.17 = (bf16[1,1024]{1,0:T(2,128)(2,1)S(1)}, bf16[1,1024]{1,0:T(2,128)(2,1)}, u32[]{:S(2)}) copy-start(bf16[1,1024]{1,0:T(2,128)(2,1)} %param.19) | copy-start | bytes 6148
  7.3 107.3 %all-gather.8.cloned.1.call-start = ((), (), s32[]{:S(2)}) async-start(), calls=%async_computation.9 | async-start | bytes 13369344 | tf_op jit(solution)/shard_map/all_gather | solution.py:145
  8.0 168.9 %all-gather.10.cloned.1.call-start = ((), (), s32[]{:S(2)}) async-start(), calls=%async_computation.10 | async-start | bytes 6684672 | tf_op jit(solution)/shard_map/all_gather | solution.py:147
  8.8 340.7 %all-gather.12.cloned.1.call-start = ((), (), s32[]{:S(2)}) async-start(), calls=%async_computation.11 | async-start | bytes 2228224 | tf_op jit(solution)/shard_map/all_gather | solution.py:150
  9.5 346.6 %all-gather.14.cloned.1.call-start = ((), (), s32[]{:S(2)}) async-start(), calls=%async_computation.12 | async-start | bytes 8912896 | tf_op jit(solution)/shard_map/all_gather | solution.py:152
  10.1 360.0 %all-gather.16.cloned.1.call-start = ((), (), s32[]{:S(2)}) async-start(), calls=%async_computation.13 | async-start | bytes 8912896 | tf_op jit(solution)/shard_map/all_gather | solution.py:154
  12.1 164.8 %copy-start.21 = (f32[512]{0:T(512)}, f32[512]{0:T(512)S(1)}, u32[]{:S(2)}) copy-start(f32[512]{0:T(512)S(1)} %broadcast_multiply_fusion.6) | copy-start | bytes 6148
  70.3 106.6 %copy-start.37 = (f32[512]{0:T(512)}, f32[512]{0:T(512)S(1)}, u32[]{:S(2)}) copy-start(f32[512]{0:T(512)S(1)} %add_rsqrt_fusion.1) | copy-start | bytes 6148
  121.5 63.3 %copy-start.19 = (f32[1,1,1,1024]{3,2,1,0:T(1,128)}, f32[1,1,1,1024]{3,2,1,0:T(1,128)S(1)}, u32[]{:S(2)}) copy-start(f32[1,1,1,1024]{3,2,1,0:T(1,128)S(1)} %get-tuple-element.313) | copy-start | bytes 12292
  121.5 63.3 %copy-start.46 = (f32[1,1,1,1024]{3,2,1,0:T(1,128)}, f32[1,1,1,1024]{3,2,1,0:T(1,128)S(1)}, u32[]{:S(2)}) copy-start(f32[1,1,1,1024]{3,2,1,0:T(1,128)S(1)} %get-tuple-element.312) | copy-start | bytes 12292
  196.1 54.0 %all-to-all-start = ((bf16[1,512,3,1024]{1,2,0,3:T(4,128)(2,1)}), bf16[1,512,3,1024]{1,2,0,3:T(4,128)(2,1)}, u32[]{:S(2)}, u32[]{:S(2)}) async-start(bf16[1,512,3,1024]{1,2,0,3:T(4,128)(2,1)} %copy.79), calls=%async_computation | async-start | bytes 8388608 | tf_op jit(solution)/shard_map/all_to_all | solution.py:179
  317.7 23.5 %all-to-all-start.1 = ((bf16[2,2,131072]{2,1,0:T(2,128)(2,1)}), bf16[2,2,131072]{2,1,0:T(2,128)(2,1)}, u32[]{:S(2)}, u32[]{:S(2)}) async-start(bf16[2,2,131072]{2,1,0:T(2,128)(2,1)} %reshape.446), calls=%async_computation.1 | async-start | bytes 2097152 | tf_op jit(solution)/shard_map/all_to_all | solution.py:192
  341.2 48.4 %copy-start.34 = (f32[16,1,256]{2,1,0:T(1,128)}, f32[16,1,256]{2,1,0:T(1,128)S(1)}, u32[]{:S(2)}) copy-start(f32[16,1,256]{2,1,0:T(1,128)S(1)} %convert_element_type.130) | copy-start | bytes 49156
  354.3 47.6 %copy-start.23 = (f32[512]{0:T(512)}, f32[512]{0:T(512)S(1)}, u32[]{:S(2)}) copy-start(f32[512]{0:T(512)S(1)} %broadcast_multiply_fusion.5) | copy-start | bytes 6148
  426.3 18.8 %all-to-all-start.2 = ((bf16[2,2,131072]{2,1,0:T(2,128)(2,1)}), bf16[2,2,131072]{2,1,0:T(2,128)(2,1)}, u32[]{:S(2)}, u32[]{:S(2)}) async-start(bf16[2,2,131072]{2,1,0:T(2,128)(2,1)} %reshape.448), calls=%async_computation.2 | async-start | bytes 2097152 | tf_op jit(solution)/shard_map/all_to_all | solution.py:236
  430.7 235.7 %reduce-scatter.10.cloned.1.call-start = ((), (), s32[]{:S(2)}) async-start(), calls=%async_computation.16 | async-start | bytes 4456448 | tf_op jit(solution)/shard_map/reduce_scatter | solution.py:293
  435.8 319.5 %reduce-scatter.8.cloned.1.call-start = ((), (), s32[]{:S(2)}) async-start(), calls=%async_computation.15 | async-start | bytes 13369344 | tf_op jit(solution)/shard_map/reduce_scatter | solution.py:290
  622.8 314.9 %reduce-scatter.12.cloned.1.call-start = ((), (), s32[]{:S(2)}) async-start(), calls=%async_computation.17 | async-start | bytes 17825792 | tf_op jit(solution)/shard_map/reduce_scatter | solution.py:221
  637.5 482.4 %reduce-scatter.14.cloned.1.call-start = ((), (), s32[]{:S(2)}) async-start(), calls=%async_computation.18 | async-start | bytes 17825792 | tf_op jit(solution)/shard_map/reduce_scatter | solution.py:223
  656.8 576.9 %all-reduce.16.cloned.1.call-start = ((), (), s32[]{:S(2)}) async-start(), calls=%async_computation.19 | async-start | bytes 6291456 | tf_op jit(solution)/shard_map/psum | solution.py:306
  666.4 455.7 %copy-start.10 = (f32[1,512,1024]{2,1,0:T(8,128)S(1)}, f32[1,512,1024]{2,1,0:T(8,128)}, u32[]{:S(2)}) copy-start(f32[1,512,1024]{2,1,0:T(8,128)} %get-tuple-element.292) | copy-start | bytes 6291460
  666.4 455.7 %copy-start.31 = (f32[1024]{0:T(1024)S(1)}, f32[1024]{0:T(1024)}, u32[]{:S(2)}) copy-start(f32[1024]{0:T(1024)} %copy-done.30) | copy-start | bytes 12292
  1120.0 340.6 %reduce-scatter.6.cloned.1.call-start = ((), (), s32[]{:S(2)}) async-start(), calls=%async_computation.14 | async-start | bytes 26738688 | tf_op jit(solution)/shard_map/reduce_scatter | solution.py:288
  1233.8 232.8 %copy-start.16 = (f32[256,1024]{1,0:T(8,128)S(1)}, f32[256,1024]{1,0:T(8,128)}, u32[]{:S(2)}) copy-start(f32[256,1024]{1,0:T(8,128)} %get-tuple-element.492) | copy-start | bytes 3145732
  (53 other events, 423.3 us)
Sparse Core Ops, SparseCore 0:
  10.4 104.1 all-gather.7
  116.8 60.0 all-gather.9
  179.1 39.9 all-gather.11
  221.2 73.6 all-gather.13
  296.9 73.1 all-gather.15
  435.9 71.3 reduce-scatter.9
  623.0 132.2 reduce-scatter.7
  759.9 177.7 reduce-scatter.11
  942.4 177.5 reduce-scatter.13
  1122.4 89.4 all-reduce.15
  1216.6 243.8 reduce-scatter.5
where the time goes:
time: 1480 us; the launch traced here: 1470 us
  waiting for transfers between devices  843 us (57%)
  matrix products  211 us (14%)
  blocking collectives  205 us (14%)
  local copies, waits for them, and re-layouts  108 us (7%)
  other arithmetic  73.9 us (5%)
  between operations  17.3 us (1%)
  starting transfers between devices  15.6 us (1%)
    reduce_scatter x1, waiting for transfers between devices, per_device(): lax.psum_scatter(mod_term, 'fsdp', scatter_dimension=0, tiled=True)  227 us
    reduce_scatter x1, waiting for transfers between devices, per_device(): lax.psum_scatter(up_term, 'fsdp', scatter_dimension=0, tiled=True)  182 us
    reduce_scatter x1, waiting for transfers between devices, per_device(): lax.psum_scatter(down_term, 'fsdp', scatter_dimension=0, tiled=True)  182 us
    unnamed x2, blocking collectives  95.9 us
    reduce_scatter x1, waiting for transfers between devices, per_device(): lax.psum_scatter(qkv_term, 'fsdp', scatter_dimension=0, tiled=True)  88.8 us
    all_gather x1, waiting for transfers between devices, per_device(): lax.all_gather(qkv_weight, 'fsdp', axis=0, tiled=True)  55.5 us
    all_to_all x1, blocking collectives, per_device(): lax.all_to_all(grad_by_heads, 'seq', split_axis=1, concat_axis=3, tiled=T...  51.4 us
    all_to_all x1, waiting for transfers between devices, per_device(): lax.all_to_all(projected, 'seq', split_axis=3, concat_axis=1, tiled=True)  48.1 us
  transfers between devices with their start and end apart: 14, of which 9 were waited for; matrix products, arithmetic and copies ran while one was open for 22% of the time, Pallas kernels for 0%

commit v1 on v0

v1 whole, which is shorter than its diff:
```python
import functools

import jax
import jax.numpy as jnp
from jax import lax
from jax.experimental import pallas as pl
from jax.experimental.pallas import tpu as pltpu
from jax.sharding import PartitionSpec as P

HD = 64


EPSILON = 1e-06


def norm_rows(values):
    centred = values - jnp.mean(values, axis=-1, keepdims=True)
    inverse = lax.rsqrt(jnp.mean(centred * centred, axis=-1, keepdims=True) + EPSILON)
    return (centred * inverse, inverse)


def norm_back(grad_normed, normed, inverse):
    mean_grad = jnp.mean(grad_normed, axis=-1, keepdims=True)
    mean_cross = jnp.mean(grad_normed * normed, axis=-1, keepdims=True)
    return inverse * (grad_normed - mean_grad - normed * mean_cross)


def project(left, weight):
    return lax.dot_general(
        left, weight, (((left.ndim - 1,), (0,)), ((), ())), preferred_element_type=jnp.float32
    )


def project_back(left, weight):
    return lax.dot_general(
        left, weight, (((left.ndim - 1,), (1,)), ((), ())), preferred_element_type=jnp.float32
    )


def weight_term(inputs, grads):
    return lax.dot_general(
        inputs, grads, (((0,), (0,)), ((), ())), preferred_element_type=jnp.float32
    )


def nt(left, right):
    return lax.dot_general(
        left, right, (((1,), (1,)), ((), ())), preferred_element_type=jnp.float32
    )


def nn(left, right):
    return jnp.dot(left, right, preferred_element_type=jnp.float32)


def forward_kernel(query_ref, key_ref, value_ref, out_ref, *, block):
    length, lanes = query_ref.shape
    factor = HD**-0.5
    for head in range(lanes // HD):
        cols = slice(head * HD, (head + 1) * HD)
        keys = key_ref[:, cols]
        values = value_ref[:, cols]

        def one_block(at, carry):
            rows = pl.ds(pl.multiple_of(at * block, block), block)
            scores = nt(query_ref[rows, cols] * factor, keys)
            exponent = jnp.exp(scores - jnp.max(scores, axis=-1, keepdims=True))
            totals = jnp.sum(exponent, axis=-1, keepdims=True)
            probs = (exponent * (1.0 / totals)).astype(jnp.bfloat16)
            out_ref[rows, cols] = nn(probs, values).astype(jnp.bfloat16)
            return carry

        lax.fori_loop(0, length // block, one_block, 0)


def backward_kernel(
    query_ref, key_ref, value_ref, grad_ref, query_grad, key_grad, value_grad, *, block
):
    length, lanes = query_ref.shape
    factor = HD**-0.5
    for head in range(lanes // HD):
        cols = slice(head * HD, (head + 1) * HD)
        keys = key_ref[:, cols]
        values = value_ref[:, cols]
        keys_turned = (keys * factor).T

        def one_block(at, carry):
            key_sum, value_sum = carry
            rows = pl.ds(pl.multiple_of(at * block, block), block)
            queries = query_ref[rows, cols] * factor
            grads = grad_ref[rows, cols]
            scores = nt(keys, queries)
            exponent = jnp.exp(scores - jnp.max(scores, axis=0, keepdims=True))
            probs = exponent * (1.0 / jnp.sum(exponent, axis=0, keepdims=True))
            grad_probs = nt(values, grads)
            cross = probs * grad_probs
            inner = jnp.sum(cross, axis=0, keepdims=True)
            grad_scores = (cross - probs * inner).astype(jnp.bfloat16)
            value_sum = value_sum + nn(probs.astype(jnp.bfloat16), grads)
            key_sum = key_sum + nn(grad_scores, queries)
            query_grad[rows, cols] = nn(keys_turned, grad_scores).T.astype(jnp.bfloat16)
            return (key_sum, value_sum)

        zeros = jnp.zeros((length, HD), jnp.float32)
        key_sum, value_sum = lax.fori_loop(0, length // block, one_block, (zeros, zeros))
        key_grad[:, cols] = key_sum.astype(jnp.bfloat16)
        value_grad[:, cols] = value_sum.astype(jnp.bfloat16)


def attend(kernel, arrays, outs, block, dots):
    count, length = arrays[0][0].shape[:2]
    part = outs[0][2]
    lanes = min(128, part)

    def spec(first):
        return pl.BlockSpec((None, length, lanes), lambda b, h, first=first: (b, 0, first + h))

    result = pl.pallas_call(
        functools.partial(kernel, block=block),
        grid=(count, part // lanes),
        in_specs=[spec(first) for _, first in arrays],
        out_specs=[spec(0) for _ in outs],
        out_shape=[jax.ShapeDtypeStruct(out, jnp.bfloat16) for out in outs],
        cost_estimate=pl.CostEstimate(
            flops=8 * dots * count * length * length * part,
            bytes_accessed=2 * count * length * part * (len(arrays) + len(outs)),
            transcendentals=count * length * length * (part // HD),
        ),
        compiler_params=pltpu.CompilerParams(vmem_limit_bytes=48 * 1024 * 1024),
    )(*[array for array, _ in arrays])
    return result


class Tokens:
    def __init__(self, size):
        self.size = size
        self.me = lax.axis_index("seq")

    def swap(self, values):
        return lax.ppermute(values, "seq", [(0, 1), (1, 0)])

    def gather(self, values):
        if self.size == 2:
            return jnp.concatenate([values, self.swap(values)], axis=1)
        return lax.all_gather(values, "seq", axis=1, tiled=True)

    def own(self, values):
        local = values.shape[1] // self.size
        if self.size == 2:
            return values[:, :local]
        return lax.dynamic_slice_in_dim(values, self.me * local, local, 1)

    def scatter(self, left, product):
        local = left.shape[1] // self.size
        if self.size == 2:
            sent = self.swap(product(left[:, local:]).astype(jnp.bfloat16))
            return product(left[:, :local]) + sent.astype(jnp.float32)
        return lax.psum_scatter(
            product(left).astype(jnp.bfloat16), "seq", scatter_dimension=1, tiled=True
        ).astype(jnp.float32)

    def to_tokens(self, values):
        local = values.shape[1] // self.size
        if self.size == 2:
            own = values[:, :local]
            other = self.swap(values[:, local:])
            first = self.me == 0
            return jnp.concatenate(
                [jnp.where(first, own, other), jnp.where(first, other, own)], axis=2
            )
        return lax.all_to_all(values, "seq", split_axis=1, concat_axis=2, tiled=True)

    def to_heads(self, values):
        part = values.shape[2] // self.size
        if self.size == 2:
            first = self.me == 0
            low, high = values[:, :, :part], values[:, :, part:]
            other = self.swap(jnp.where(first, high, low))
            return jnp.concatenate([jnp.where(first, low, high), other], axis=1)
        return lax.all_to_all(values, "seq", split_axis=2, concat_axis=1, tiled=True)


def gather_rows(shard):
    return lax.all_gather(shard, "fsdp", axis=0, tiled=True)


def scatter_rows(term):
    return lax.psum_scatter(term.astype(jnp.bfloat16), "fsdp", scatter_dimension=0, tiled=True)


def gelu_parts(value):
    return jax.vjp(lambda v: jax.nn.gelu(v, approximate=True), value)


def per_device(
    fsdp,
    seq,
    latents,
    conditioning,
    mod_weight,
    mod_bias,
    qkv_weight,
    query_bias,
    value_bias,
    out_weight,
    out_bias,
    up_weight,
    up_bias,
    down_weight,
    down_bias,
    cotangent,
):
    f32 = jnp.float32
    count, local_len, width = latents.shape
    length = local_len * seq
    hidden = up_weight.shape[1]
    part = width // seq
    unit = hidden // (fsdp * seq)
    mine = lax.axis_index("seq")
    owner = lax.axis_index("fsdp")
    tokens = Tokens(seq)
    mod_rows = mod_weight.shape[0]

    cond_float = conditioning.astype(f32)
    silu_local = jax.nn.silu(cond_float).astype(jnp.bfloat16)
    small = jnp.concatenate(
        [silu_local.reshape(-1), query_bias, value_bias, out_bias, up_bias, down_bias]
    )
    small = lax.all_gather(small, "fsdp", axis=0)
    cuts = [count * width]
    for vector in (query_bias, value_bias, out_bias, up_bias, down_bias):
        cuts.append(cuts[-1] + vector.shape[0])
    silu_all = small[:, : cuts[0]].reshape(fsdp * count, width)
    full_query_bias, full_value_bias, full_out_bias, full_up_bias, full_down_bias = (
        small[:, start:stop].reshape(-1).astype(f32) for start, stop in zip(cuts, cuts[1:])
    )

    qkv_shard = lax.dynamic_slice_in_dim(
        qkv_weight.reshape(-1, 3, width), mine * part, part, 2
    ).reshape(-1, 3 * part)
    part_qkv = gather_rows(qkv_shard)
    full_out = gather_rows(out_weight)
    up_shard = lax.dynamic_index_in_dim(
        up_weight.reshape(-1, fsdp, seq, unit), mine, 2, keepdims=False
    ).reshape(-1, fsdp * unit)
    part_up = gather_rows(up_shard)
    part_down = gather_rows(lax.dynamic_slice_in_dim(down_weight, mine * unit, unit, 0))
    part_up_bias = lax.dynamic_index_in_dim(
        full_up_bias.reshape(fsdp, seq, unit), mine, 1, keepdims=False
    ).reshape(-1)

    silu_rows = lax.dynamic_slice_in_dim(silu_all, owner * mod_rows, mod_rows, 1)
    mod_term = project(silu_rows, mod_weight)
    columns = mod_bias.shape[0]
    placed = lax.dynamic_update_slice_in_dim(
        jnp.zeros((6 * width,), f32), mod_bias.astype(f32), owner * columns, 0
    )
    modulation = lax.psum_scatter(
        mod_term + placed, "fsdp", scatter_dimension=0, tiled=True
    ).reshape(count, 6, 1, width)
    shift_one = modulation[:, 0]
    scale_one = modulation[:, 1]
    gate_one = modulation[:, 2]
    shift_two = modulation[:, 3]
    scale_two = modulation[:, 4]
    gate_two = modulation[:, 5]

    all_latents = tokens.gather(latents)
    all_cotangent = tokens.gather(cotangent)
    normed_one, _ = norm_rows(all_latents.astype(f32))
    attn_input = (normed_one * (1.0 + scale_one) + shift_one).astype(jnp.bfloat16)
    bias_part = jnp.concatenate(
        [
            lax.dynamic_slice_in_dim(full_query_bias, mine * part, part, 0),
            jnp.zeros((part,), f32),
            lax.dynamic_slice_in_dim(full_value_bias, mine * part, part, 0),
        ]
    )
    by_heads = (project(attn_input, part_qkv) + bias_part).astype(jnp.bfloat16)
    groups = part // min(128, part)
    streams = [(by_heads, 0), (by_heads, groups), (by_heads, 2 * groups)]
    block = min(256, length)
    head_shape = (count, length, part)
    (mixed,) = attend(forward_kernel, streams, [head_shape], block, 2)
    attn_heads = tokens.to_tokens(mixed)
    inputs = latents.astype(f32)
    attn_out = project(attn_heads, full_out) + full_out_bias
    after_attn = inputs + gate_one * attn_out
    normed_two, inverse_two = norm_rows(after_attn)
    mlp_local = (normed_two * (1.0 + scale_two) + shift_two).astype(jnp.bfloat16)
    mlp_input = tokens.gather(mlp_local)
    hidden_pre = project(mlp_input, part_up) + part_up_bias
    grad_branch = (gate_two * all_cotangent.astype(f32)).astype(jnp.bfloat16)
    hidden_act, gelu_back = gelu_parts(hidden_pre)
    hidden_act = hidden_act.astype(jnp.bfloat16)
    grad_act = project_back(grad_branch, part_down)
    grad_pre = gelu_back(grad_act)[0].astype(jnp.bfloat16)
    grad_mlp_in = tokens.scatter(grad_pre, lambda rows: project_back(rows, part_up))

    rows = count * length
    flat_branch = grad_branch.reshape(rows, width)
    flat_pre = grad_pre.reshape(rows, -1)
    down_part = scatter_rows(weight_term(hidden_act.reshape(rows, -1), flat_branch))
    up_part = scatter_rows(weight_term(mlp_input.reshape(rows, width), flat_pre))
    up_bias_term = jnp.sum(flat_pre.astype(f32), axis=0)
    own_branch = tokens.own(grad_branch)
    down_bias_term = jnp.sum(own_branch.astype(f32), axis=(0, 1))

    branch_out = tokens.scatter(hidden_act, lambda rows: project(rows, part_down)) + full_down_bias
    block_output = (after_attn + gate_two * branch_out).astype(jnp.bfloat16)
    grad_out = cotangent.astype(f32)
    grad_gate_two = jnp.sum(grad_out * branch_out, axis=1)

    grad_scale_two = jnp.sum(grad_mlp_in * normed_two, axis=1)
    grad_shift_two = jnp.sum(grad_mlp_in, axis=1)
    grad_after = grad_out + norm_back(grad_mlp_in * (1.0 + scale_two), normed_two, inverse_two)
    grad_attn = (gate_one * grad_after).astype(jnp.bfloat16)
    grad_gate_one = jnp.sum(grad_after * attn_out, axis=1)
    grad_heads = project_back(grad_attn, full_out).astype(jnp.bfloat16)
    grad_mixed = tokens.to_heads(grad_heads)
    flat_attn = grad_attn.reshape(count * local_len, width)
    out_part = scatter_rows(weight_term(attn_heads.reshape(count * local_len, width), flat_attn))
    out_bias_term = jnp.sum(flat_attn.astype(f32), axis=0)

    grads = attend(
        backward_kernel, streams + [(grad_mixed, 0)], [head_shape] * 3, block, 5
    )
    grad_projected = jnp.concatenate(grads, axis=2)
    flat_projected = grad_projected.reshape(rows, 3 * part)
    qkv_part = scatter_rows(weight_term(attn_input.reshape(rows, width), flat_projected))
    column_sums = jnp.sum(flat_projected.astype(f32), axis=0)
    grad_attn_in = tokens.scatter(grad_projected, lambda rows: project_back(rows, part_qkv))
    own_normed, own_inverse = norm_rows(inputs)
    grad_scale_one = jnp.sum(grad_attn_in * own_normed, axis=1)
    grad_shift_one = jnp.sum(grad_attn_in, axis=1)
    latents_grad = grad_after + norm_back(
        grad_attn_in * (1.0 + scale_one), own_normed, own_inverse
    )

    early = jnp.concatenate(
        [
            jnp.concatenate(
                [grad_gate_one, grad_shift_two, grad_scale_two, grad_gate_two], axis=1
            ).reshape(-1),
            out_bias_term,
            down_bias_term,
            up_bias_term,
        ]
    )
    early = lax.all_gather(early, ("fsdp", "seq"), axis=0).reshape(fsdp, seq, -1)
    late = jnp.concatenate(
        [
            jnp.concatenate([grad_shift_one, grad_scale_one], axis=1).reshape(-1),
            column_sums[:part],
            column_sums[2 * part :],
        ]
    )
    late = lax.all_gather(late, ("fsdp", "seq"), axis=0).reshape(fsdp, seq, -1)
    at = count * 4 * width
    early_mod = jnp.sum(early[:, :, :at], axis=1).reshape(fsdp * count, 4 * width)
    early_bias = jnp.sum(early[:, :, at : at + 2 * width], axis=(0, 1))
    out_bias_total = lax.dynamic_slice_in_dim(
        early_bias[:width], owner * out_bias.shape[0], out_bias.shape[0], 0
    )
    down_bias_total = lax.dynamic_slice_in_dim(
        early_bias[width:], owner * down_bias.shape[0], down_bias.shape[0], 0
    )
    up_bias_all = early[:, :, at + 2 * width :].reshape(fsdp, seq, fsdp, unit)
    up_bias_total = jnp.sum(
        lax.dynamic_index_in_dim(up_bias_all, owner, 2, keepdims=False), axis=0
    ).reshape(-1)
    at = count * 2 * width
    late_mod = jnp.sum(late[:, :, :at], axis=1).reshape(fsdp * count, 2 * width)
    late_bias = jnp.sum(late[:, :, at:], axis=0).reshape(seq, 2, part)
    query_bias_total = lax.dynamic_slice_in_dim(
        late_bias[:, 0].reshape(-1), owner * query_bias.shape[0], query_bias.shape[0], 0
    )
    value_bias_total = lax.dynamic_slice_in_dim(
        late_bias[:, 1].reshape(-1), owner * value_bias.shape[0], value_bias.shape[0], 0
    )
    grad_modulation = jnp.concatenate([late_mod, early_mod], axis=1).astype(jnp.bfloat16)
    mod_total = weight_term(silu_rows, grad_modulation)
    mod_bias_total = jnp.sum(
        lax.dynamic_slice_in_dim(grad_modulation, owner * columns, columns, 1).astype(f32), axis=0
    )
    grad_silu_rows = project_back(grad_modulation, mod_weight)
    grad_silu_all = lax.all_gather(grad_silu_rows, "fsdp", axis=1, tiled=True)
    grad_silu = lax.dynamic_slice_in_dim(grad_silu_all, owner * count, count, 0)
    _, silu_back = jax.vjp(jax.nn.silu, cond_float)
    conditioning_grad = silu_back(grad_silu)[0]

    down_total = lax.all_gather(down_part, "seq", axis=0, tiled=True).astype(f32)
    up_total = (
        lax.all_gather(up_part.reshape(-1, fsdp, 1, unit), "seq", axis=2, tiled=True)
        .reshape(-1, hidden)
        .astype(f32)
    )
    qkv_total = (
        lax.all_gather(qkv_part.reshape(-1, 3, part), "seq", axis=2, tiled=True)
        .reshape(-1, 3 * width)
        .astype(f32)
    )
    out_total = lax.psum(out_part.astype(f32), "seq")
    return (
        block_output,
        latents_grad,
        conditioning_grad,
        mod_total,
        mod_bias_total,
        qkv_total,
        query_bias_total,
        value_bias_total,
        out_total,
        out_bias_total,
        up_total,
        up_bias_total,
        down_total,
        down_bias_total,
    )


def solution(mesh):
    return jax.shard_map(
        functools.partial(per_device, mesh.shape["fsdp"], mesh.shape["seq"]),
        mesh=mesh,
        in_specs=(
            P("fsdp", "seq", None),
            P("fsdp", None),
            P("fsdp", None),
            P("fsdp"),
            P("fsdp", None),
            P("fsdp"),
            P("fsdp"),
            P("fsdp", None),
            P("fsdp"),
            P("fsdp", None),
            P("fsdp"),
            P("fsdp", None),
            P("fsdp"),
            P("fsdp", "seq", None),
        ),
        out_specs=(
            P("fsdp", "seq", None),
            P("fsdp", "seq", None),
            P("fsdp", None),
            P("fsdp", None),
            P("fsdp"),
            P("fsdp", None),
            P("fsdp"),
            P("fsdp"),
            P("fsdp", None),
            P("fsdp"),
            P("fsdp", None),
            P("fsdp"),
            P("fsdp", None),
            P("fsdp"),
        ),
        check_vma=False,
    )
```

time: 1480 us -> 753 us (0.51)
  waiting for transfers between devices: 843 us -> 341 us
  matrix products: 211 us -> 101 us
  Pallas kernels: 0 us -> 81.7 us
  local copies, waits for them, and re-layouts: 108 us -> 29.8 us
  blocking collectives: 205 us -> 145 us
  other arithmetic: 73.9 us -> 23.4 us
    reduce_scatter x5 -> x4, waiting for transfers between devices: 680 us -> 68.9 us  [scatter_rows(): lax.psum_scatter(term.astype(jnp.bfloat16), 'fsdp', scatter_dimension=0,...]
    ppermute x0 -> x8, waiting for transfers between devices: none -> 100 us  [swap(): return lax.ppermute(values, 'seq', [(0, 1), (1, 0)])]
    unnamed x2 -> x0, blocking collectives: 95.9 us -> none
    all_gather x2 -> x6, blocking collectives: 36.7 us -> 132 us  [the longest x1 68.3 us: per_device(): late = lax.all_gather(late, ('fsdp', 'seq'), axis=0).reshape(fsdp, seq, -1)]
    pallas_call x0 -> x2, Pallas kernels: none -> 81.7 us  [attend(): pl.pallas_call(functools.partial(kernel, block=block), grid=(count, part...]
    dot_general x14 -> x0, matrix products: 81.4 us -> none  [the longest x2 21.9 us: one_block(): jnp.einsum('qhd,khd->hqk', grad_block, values, preferred_element_type=jnp...]
    unnamed x11, waiting for transfers between devices: 3.21 us -> 78.9 us
    all_to_all x3 -> x0, waiting for transfers between devices: 57.4 us -> none  [the longest x1 48.1 us: per_device(): lax.all_to_all(projected, 'seq', split_axis=3, concat_axis=1, tiled=True)]
  transfers between devices with their start and end apart: 14 -> 18, of which waited for: 9 -> 13; matrix products, arithmetic and copies ran while one was open for 22% -> 15% of each run, Pallas kernels for 0% -> 11%
where the time goes in v1:
time: 753 us; the launch traced here: 749 us
  waiting for transfers between devices  341 us (45%)
  blocking collectives  145 us (19%)
  matrix products  101 us (13%)
  Pallas kernels  81.7 us (11%)
  local copies, waits for them, and re-layouts  29.8 us (4%)
  other arithmetic  23.4 us (3%)
  between operations  15 us (2%)
  starting transfers between devices  11 us (1%)
    ppermute x8, waiting for transfers between devices, swap(): return lax.ppermute(values, 'seq', [(0, 1), (1, 0)])  100 us
    all_gather x4, waiting for transfers between devices, gather_rows(): return lax.all_gather(shard, 'fsdp', axis=0, tiled=True)  93.5 us
    pallas_call x2, Pallas kernels, attend(): pl.pallas_call(functools.partial(kernel, block=block), grid=(count, part...  81.7 us
    unnamed x11, waiting for transfers between devices  78.9 us
    reduce_scatter x4, waiting for transfers between devices, scatter_rows(): lax.psum_scatter(term.astype(jnp.bfloat16), 'fsdp', scatter_dimension=0,...  68.9 us
    all_gather x1, blocking collectives, per_device(): late = lax.all_gather(late, ('fsdp', 'seq'), axis=0).reshape(fsdp, seq, -1)  68.3 us
    dot_general x7, matrix products, project_back(): lax.dot_general(left, weight, (((left.ndim - 1,), (1,)), ((), ())), prefe...  36.9 us
    dot_general x6, matrix products, project(): lax.dot_general(left, weight, (((left.ndim - 1,), (0,)), ((), ())), prefe...  32.5 us
  transfers between devices with their start and end apart: 18, of which 13 were waited for; matrix products, arithmetic and copies ran while one was open for 15% of the time, Pallas kernels for 11%

profile of v1, /device:TPU:0, one launch (start us, length us, event | category | flops | bytes accessed | tf_op | source)
XLA Modules:
  0.0 748.8 jit_solution(6101928080188127055)
XLA Ops:
  12.1 23.3 %all-gather.3 = bf16[16,1,1536]{2,1,0:T(2,128)(2,1)S(1)} all-gather(bf16[1,1,1536]{2,1,0:T(2,128)(2,1)S(1)} %reshape.604), channel_id=2, replica_groups=mesh['fsdp'=16,'seq'=2] {'fsdp'}, dimensions={0}, use_global_device_ids=true | all-gather | bytes 52224 | tf_op jit(solution)/shard_map/all_gather | solution.py:229
  47.1 78.1 %all-reduce.4.cloned.1.call-done = f32[16,6144]{1,0:T(8,128)} async-done(((f32[16,6144]{1,0:T(8,128)}), f32[16,6144]{1,0:T(8,128)}) %all-reduce.4.cloned.1.call-update) | async-done | bytes 393232
  127.9 44.6 %all-gather.11.cloned.1.call-done = bf16[1024,1536]{1,0:T(8,128)(2,1)} async-done(((bf16[64,1536]{1,0:T(8,128)(2,1)}), bf16[1024,1536]{1,0:T(8,128)(2,1)}) %all-gather.11.cloned.1.call-update) | async-done | bytes 3145744 | tf_op jit(solution)/shard_map/all_gather | solution.py:184
  179.4 30.2 %shard_map.245 = bf16[1,1024,512]{2,1,0:T(8,128)(2,1)S(1)} custom-call(bf16[1,1024,1536]{2,1,0:T(8,128)(2,1)S(1)} %fusion.9.query_ref.key_ref.value_ref, bf16[1,1024,1536]{2,1,0:T(8,128)(2,1)S(1)} %fusion.9.query_ref.key_ref.value_ref, bf16[1,1024,1536]{2,1,0:T(8,128)(2,1)S(1)} %fusion.9.query_ref.key_ref.value_ref), custom_call_target="tpu_custom_call" | custom-call | flops 8589934592 | bytes 4194304 | tf_op jit(solution)/shard_map/pallas_call | solution.py:118
  211.5 12.4 %collective-permute-done.1 = bf16[1,512,512]{2,1,0:T(8,128)(2,1)} collective-permute-done((bf16[1,512,512]{2,1,0:T(8,128)(2,1)S(1)}, bf16[1,512,512]{2,1,0:T(8,128)(2,1)}, u32[]{:S(2)}, u32[]{:S(2)}) %collective-permute-start.1) | collective-permute-done | bytes 524320 | tf_op jit(solution)/shard_map/ppermute | solution.py:140
  234.5 24.1 %collective-permute-done.2 = bf16[1,512,1024]{2,1,0:T(8,128)(2,1)} collective-permute-done((bf16[1,512,1024]{2,1,0:T(8,128)(2,1)S(1)}, bf16[1,512,1024]{2,1,0:T(8,128)(2,1)}, u32[]{:S(2)}, u32[]{:S(2)}) %collective-permute-start.2) | collective-permute-done | bytes 1048608 | tf_op jit(solution)/shard_map/ppermute | solution.py:140
  258.6 8.9 %all-gather.15.cloned.1.call-done = bf16[1024,2048]{1,0:T(8,128)(2,1)} async-done(((bf16[64,2048]{1,0:T(8,128)(2,1)}), bf16[1024,2048]{1,0:T(8,128)(2,1)}) %all-gather.15.cloned.1.call-update) | async-done | bytes 4194320 | tf_op jit(solution)/shard_map/all_gather | solution.py:184
  267.5 10.2 %fusion.37 = f32[1024,2048]{1,0:T(8,128)} fusion(bf16[1024,2048]{1,0:T(8,128)(2,1)} %all-gather.15.cloned.1.call-done, bf16[1,512,1024]{2,1,0:T(8,128)(2,1)} %collective-permute-done.2, bf16[1,512,1024]{2,1,0:T(8,128)(2,1)S(1)} %add_convert_fusion.3), kind=kOutput, calls=%fused_computation.82 | convolution fusion | flops 4299161600 | bytes 14680064 | tf_op jit(solution)/shard_map/dot_general | solution.py:29
  279.4 40.0 %all-gather.17.cloned.1.call-done = bf16[2048,1024]{1,0:T(8,128)(2,1)} async-done(((bf16[128,1024]{1,0:T(8,128)(2,1)}), bf16[2048,1024]{1,0:T(8,128)(2,1)}) %all-gather.17.cloned.1.call-update) | async-done | bytes 4194320 | tf_op jit(solution)/shard_map/all_gather | solution.py:184
  319.4 13.4 %convert_reduce_fusion = (f32[2048]{0:T(1024)S(1)}, bf16[1024,2048]{1,0:T(8,128)(2,1)S(1)}) fusion(f32[1024,2048]{1,0:T(8,128)} %fusion.37, f32[2048]{0:T(1024)S(1)} %bitcast.172, bf16[2048,1024]{1,0:T(8,128)(2,1)} %all-gather.17.cloned.1.call-done, bf16[512,1024]{1,0:T(8,128)(2,1)} %bitcast.19, bf16[512,1024]{1,0:T(8,128)(2,1)} %bitcast.18, ...), kind=kOutput, calls=%fused_computation.9 | convolution fusion | flops 4349491200 | bytes 18894848 | tf_op jit(solution)/shard_map/dot_general | solution.py:35
  346.9 17.5 %collective-permute-done.5 = bf16[1,512,1024]{2,1,0:T(8,128)(2,1)} collective-permute-done((bf16[1,512,1024]{2,1,0:T(8,128)(2,1)}, bf16[1,512,1024]{2,1,0:T(8,128)(2,1)}, u32[]{:S(2)}, u32[]{:S(2)}) %collective-permute-start.5) | collective-permute-done | bytes 1048608 | tf_op jit(solution)/shard_map/ppermute | solution.py:140
  371.1 15.0 %collective-permute-done.3 = bf16[1,512,1024]{2,1,0:T(8,128)(2,1)S(1)} collective-permute-done((bf16[1,512,1024]{2,1,0:T(8,128)(2,1)}, bf16[1,512,1024]{2,1,0:T(8,128)(2,1)S(1)}, u32[]{:S(2)}, u32[]{:S(2)}) %collective-permute-start.3) | collective-permute-done | bytes 1048608 | tf_op jit(solution)/shard_map/ppermute | solution.py:140
  402.9 9.7 %collective-permute-done.6 = bf16[1,512,512]{2,1,0:T(8,128)(2,1)} collective-permute-done((bf16[1,512,512]{2,1,0:T(8,128)(2,1)}, bf16[1,512,512]{2,1,0:T(8,128)(2,1)}, u32[]{:S(2)}, u32[]{:S(2)}) %collective-permute-start.6) | collective-permute-done | bytes 524320 | tf_op jit(solution)/shard_map/ppermute | solution.py:140
  413.7 51.4 %shard_map.246 = (bf16[1,1024,512]{2,1,0:T(8,128)(2,1)S(1)}, bf16[1,1024,512]{2,1,0:T(8,128)(2,1)S(1)}, bf16[1,1024,512]{2,1,0:T(8,128)(2,1)S(1)}) custom-call(bf16[1,1024,1536]{2,1,0:T(8,128)(2,1)} %copy-done.1, bf16[1,1024,1536]{2,1,0:T(8,128)(2,1)} %copy-done.1, bf16[1,1024,1536]{2,1,0:T(8,128)(2,1)} %copy-done.1, ...), custom_call_target="tpu_custom_call" | custom-call | flops 21474836480 | bytes 7340032 | tf_op jit(solution)/shard_map/pallas_call | solution.py:118
  473.5 9.0 %convolution_convert_fusion.2 = bf16[1024,2048]{1,0:T(8,128)(2,1)} fusion(bf16[1024,2048]{1,0:T(8,128)(2,1)} %copy-done.26, bf16[1,512,1024]{2,1,0:T(8,128)(2,1)} %collective-permute-done.2, bf16[1,512,1024]{2,1,0:T(8,128)(2,1)S(1)} %copy-done.14), kind=kOutput, calls=%fused_computation.22 | convolution fusion | flops 4301258752 | bytes 10485760 | tf_op jit(solution)/shard_map/dot_general | solution.py:41
  482.8 12.7 %convolution_convert_fusion.1 = bf16[2048,1024]{1,0:T(8,128)(2,1)} fusion(bf16[512,1024]{1,0:T(8,128)(2,1)} %bitcast.19, bf16[512,1024]{1,0:T(8,128)(2,1)} %bitcast.18, f32[1024]{0:T(1024)S(1)} %bitcast.187, f32[1024,2048]{1,0:T(8,128)} %fusion.37, f32[2048]{0:T(1024)S(1)} %bitcast.174), kind=kOutput, calls=%fused_computation.21 | convolution fusion | flops 4324327424 | bytes 14692352 | tf_op jit(solution)/shard_map/dot_general | solution.py:41
  503.8 19.7 %collective-permute-done.7 = bf16[1,512,1024]{2,1,0:T(8,128)(2,1)} collective-permute-done((bf16[1,512,1024]{2,1,0:T(8,128)(2,1)S(1)}, bf16[1,512,1024]{2,1,0:T(8,128)(2,1)}, u32[]{:S(2)}, u32[]{:S(2)}) %collective-permute-start.7) | collective-permute-done | bytes 1048608 | tf_op jit(solution)/shard_map/ppermute | solution.py:140
  529.5 68.3 %all-gather.1 = f32[98304]{0:T(1024)S(1)} all-gather(f32[3072]{0:T(1024)S(1)} %pad_maximum_fusion.8), channel_id=3, replica_groups=mesh['fsdp'=16,'seq'=2] {'fsdp','seq'}, dimensions={0}, use_global_device_ids=true | all-gather | bytes 405504 | tf_op jit(solution)/shard_map/all_gather | solution.py:358
  607.6 18.0 %all-gather.4 = f32[16,64,16]{1,2,0:T(8,128)S(1)} all-gather(f32[1,64,16]{1,2,0:T(8,128)S(1)} %convolution_bitcast_fusion), channel_id=1, replica_groups=mesh['fsdp'=16,'seq'=2] {'fsdp'}, dimensions={0}, use_global_device_ids=true | all-gather | bytes 69632 | tf_op jit(solution)/shard_map/all_gather | solution.py:387
  630.4 13.1 %all-reduce.5 = f32[64,1024]{1,0:T(8,128)} all-reduce(bf16[64,1024]{1,0:T(8,128)(2,1)} %reduce-scatter.7.cloned.1.call-done), channel_id=1, replica_groups=mesh['fsdp'=16,'seq'=2] {'seq'}, use_global_device_ids=true, to_apply=%region_27.28 | all-reduce | flops 65536 | bytes 393216 | tf_op jit(solution)/shard_map/psum | solution.py:403
  644.6 8.0 %all_gather.53 = bf16[64,3,1024]{2,1,0:T(4,128)(2,1)S(1)} all-gather(bf16[64,3,512]{2,1,0:T(4,128)(2,1)S(1)} %reshape.587), channel_id=1, replica_groups=mesh['fsdp'=16,'seq'=2] {'seq'}, dimensions={2}, use_global_device_ids=true | all-gather | bytes 589824 | tf_op jit(solution)/shard_map/all_gather | solution.py:399
  658.5 7.4 all_gather.54
  668.2 65.1 %reduce-scatter.11.cloned.1.call-done = bf16[128,1024]{1,0:T(8,128)(2,1)} async-done(((bf16[2048,1024]{1,0:T(8,128)(2,1)}), bf16[128,1024]{1,0:T(8,128)(2,1)}) %reduce-scatter.11.cloned.1.call-update) | async-done | bytes 262160 | tf_op jit(solution)/shard_map/reduce_scatter | solution.py:188
  733.4 7.2 all_gather.55
  (194 shorter events, 126.4 us)
Async XLA Ops:
  7.2 118.0 %all-reduce.4.cloned.1.call-start = ((), (), s32[]{:S(2)}) async-start(), calls=%async_computation.13 | async-start | bytes 786432
  37.3 135.2 %all-gather.11.cloned.1.call-start = ((), (), s32[]{:S(2)}) async-start(), calls=%async_computation.4 | async-start | bytes 3342336 | tf_op jit(solution)/shard_map/all_gather | solution.py:184
  40.0 185.9 %all-gather.13.cloned.1.call-start = ((), (), s32[]{:S(2)}) async-start(), calls=%async_computation.5 | async-start | bytes 2228224 | tf_op jit(solution)/shard_map/all_gather | solution.py:184
  40.7 226.7 %all-gather.15.cloned.1.call-start = ((), (), s32[]{:S(2)}) async-start(), calls=%async_computation.6 | async-start | bytes 4456448 | tf_op jit(solution)/shard_map/all_gather | solution.py:184
  43.5 275.9 %all-gather.17.cloned.1.call-start = ((), (), s32[]{:S(2)}) async-start(), calls=%async_computation.7 | async-start | bytes 4456448 | tf_op jit(solution)/shard_map/all_gather | solution.py:184
  44.3 559.7 %all-gather.19.cloned.1.call-start = ((), (), s32[]{:S(2)}) async-start(), calls=%async_computation.12 | async-start | bytes 1081344 | tf_op jit(solution)/shard_map/all_gather | solution.py:350
  44.5 82.3 %collective-permute-start = (bf16[1,512,1024]{2,1,0:T(8,128)(2,1)S(1)}, bf16[1,512,1024]{2,1,0:T(8,128)(2,1)S(1)}, u32[]{:S(2)}, u32[]{:S(2)}) collective-permute-start(bf16[1,512,1024]{2,1,0:T(8,128)(2,1)S(1)} %copy-done.2), channel_id=1, source_target_pairs={{0,1},{1,0},{2,3},{3,2},{4,5},{5,4},{6,7},{7,6},{8,9},{9,8},{10,11... | collective-permute-start | bytes 3145736 | tf_op jit(solution)/shard_map/ppermute | solution.py:140
  126.9 45.7 %copy-start.9 = (bf16[1,512,1024]{2,1,0:T(8,128)(2,1)}, bf16[1,512,1024]{2,1,0:T(8,128)(2,1)S(1)}, u32[]{:S(2)}) copy-start(bf16[1,512,1024]{2,1,0:T(8,128)(2,1)S(1)} %collective-permute-done) | copy-start | bytes 3145732
  209.7 14.2 %collective-permute-start.1 = (bf16[1,512,512]{2,1,0:T(8,128)(2,1)S(1)}, bf16[1,512,512]{2,1,0:T(8,128)(2,1)}, u32[]{:S(2)}, u32[]{:S(2)}) collective-permute-start(bf16[1,512,512]{2,1,0:T(8,128)(2,1)S(1)} %slice.143), channel_id=1, source_target_pairs={{0,1},{1,0},{2,3},{3,2},{4,5},{5,4},{6,7},{7,6},{8,9},{9,8},{10,11... | collective-permute-start | bytes 1572872 | tf_op jit(solution)/shard_map/ppermute | solution.py:140
  232.3 45.4 %copy-start.13 = (bf16[1,512,1024]{2,1,0:T(8,128)(2,1)}, bf16[1,512,1024]{2,1,0:T(8,128)(2,1)S(1)}, u32[]{:S(2)}) copy-start(bf16[1,512,1024]{2,1,0:T(8,128)(2,1)S(1)} %add_convert_fusion.3) | copy-start | bytes 3145732
  232.3 26.3 %collective-permute-start.2 = (bf16[1,512,1024]{2,1,0:T(8,128)(2,1)S(1)}, bf16[1,512,1024]{2,1,0:T(8,128)(2,1)}, u32[]{:S(2)}, u32[]{:S(2)}) collective-permute-start(bf16[1,512,1024]{2,1,0:T(8,128)(2,1)S(1)} %add_convert_fusion.3), channel_id=1, source_target_pairs={{0,1},{1,0},{2,3},{3,2},{4,5},{5,4},{6,7},{7,6},{8,9},{9,8},{10,11... | collective-permute-start | bytes 3145736 | tf_op jit(solution)/shard_map/ppermute | solution.py:140
  233.8 45.6 %collective-permute-start.4 = (bf16[1,512,1024]{2,1,0:T(8,128)(2,1)}, bf16[1,512,1024]{2,1,0:T(8,128)(2,1)}, u32[]{:S(2)}, u32[]{:S(2)}) collective-permute-start(bf16[1,512,1024]{2,1,0:T(8,128)(2,1)} %param.27), channel_id=1, source_target_pairs={{0,1},{1,0},{2,3},{3,2},{4,5},{5,4},{6,7},{7,6},{8,9},{9,8},{10,11... | collective-permute-start | bytes 3145736 | tf_op jit(solution)/shard_map/ppermute | solution.py:140
  338.1 26.3 %collective-permute-start.5 = (bf16[1,512,1024]{2,1,0:T(8,128)(2,1)}, bf16[1,512,1024]{2,1,0:T(8,128)(2,1)}, u32[]{:S(2)}, u32[]{:S(2)}) collective-permute-start(bf16[1,512,1024]{2,1,0:T(8,128)(2,1)} %fusion.33), channel_id=1, source_target_pairs={{0,1},{1,0},{2,3},{3,2},{4,5},{5,4},{6,7},{7,6},{8,9},{9,8},{10,11... | collective-permute-start | bytes 3145736 | tf_op jit(solution)/shard_map/ppermute | solution.py:140
  346.3 39.8 %collective-permute-start.3 = (bf16[1,512,1024]{2,1,0:T(8,128)(2,1)}, bf16[1,512,1024]{2,1,0:T(8,128)(2,1)S(1)}, u32[]{:S(2)}, u32[]{:S(2)}) collective-permute-start(bf16[1,512,1024]{2,1,0:T(8,128)(2,1)} %fusion.34), channel_id=1, source_target_pairs={{0,1},{1,0},{2,3},{3,2},{4,5},{5,4},{6,7},{7,6},{8,9},{9,8},{10,11... | collective-permute-start | bytes 3145736 | tf_op jit(solution)/shard_map/ppermute | solution.py:140
  346.9 39.2 %copy-start.5 = (f32[1,512,1024]{2,1,0:T(8,128)S(1)}, f32[1,512,1024]{2,1,0:T(8,128)}, u32[]{:S(2)}) copy-start(f32[1,512,1024]{2,1,0:T(8,128)} %copy-done.4) | copy-start | bytes 6291460
  346.9 39.2 %copy-start.12 = (bf16[1,1024,2048]{2,1,0:T(8,128)(2,1)S(1)}, bf16[1,1024,2048]{2,1,0:T(8,128)(2,1)}, u32[]{:S(2)}) copy-start(bf16[1,1024,2048]{2,1,0:T(8,128)(2,1)} %copy-done.11) | copy-start | bytes 12582916
  346.9 39.2 %copy-start.25 = (bf16[2048,1024]{1,0:T(8,128)(2,1)S(1)}, bf16[2048,1024]{1,0:T(8,128)(2,1)}, u32[]{:S(2)}) copy-start(bf16[2048,1024]{1,0:T(8,128)(2,1)} %all-gather.17.cloned.1.call-done) | copy-start | bytes 12582916
  346.9 39.2 %copy-start.28 = (f32[512,1024]{1,0:T(8,128)S(1)}, f32[512,1024]{1,0:T(8,128)}, u32[]{:S(2)}) copy-start(f32[512,1024]{1,0:T(8,128)} %get-tuple-element.64) | copy-start | bytes 6291460
  394.8 235.6 %reduce-scatter.7.cloned.1.call-start = ((), (), s32[]{:S(2)}) async-start(), calls=%async_computation.9 | async-start | bytes 2228224 | tf_op jit(solution)/shard_map/reduce_scatter | solution.py:188
  398.7 13.8 %collective-permute-start.6 = (bf16[1,512,512]{2,1,0:T(8,128)(2,1)}, bf16[1,512,512]{2,1,0:T(8,128)(2,1)}, u32[]{:S(2)}, u32[]{:S(2)}) collective-permute-start(bf16[1,512,512]{2,1,0:T(8,128)(2,1)} %get-tuple-element.47), channel_id=1, source_target_pairs={{0,1},{1,0},{2,3},{3,2},{4,5},{5,4},{6,7},{7,6},{8,9},{9,8},{10,11... | collective-permute-start | bytes 1572872 | tf_op jit(solution)/shard_map/ppermute | solution.py:140
  402.8 240.7 %reduce-scatter.5.cloned.1.call-start = ((), (), s32[]{:S(2)}) async-start(), calls=%async_computation.8 | async-start | bytes 3342336 | tf_op jit(solution)/shard_map/reduce_scatter | solution.py:188
  472.3 185.2 %reduce-scatter.9.cloned.1.call-start = ((), (), s32[]{:S(2)}) async-start(), calls=%async_computation.10 | async-start | bytes 4456448 | tf_op jit(solution)/shard_map/reduce_scatter | solution.py:188
  482.5 250.8 %reduce-scatter.11.cloned.1.call-start = ((), (), s32[]{:S(2)}) async-start(), calls=%async_computation.11 | async-start | bytes 4456448 | tf_op jit(solution)/shard_map/reduce_scatter | solution.py:188
  499.7 23.8 %collective-permute-start.7 = (bf16[1,512,1024]{2,1,0:T(8,128)(2,1)S(1)}, bf16[1,512,1024]{2,1,0:T(8,128)(2,1)}, u32[]{:S(2)}, u32[]{:S(2)}) collective-permute-start(bf16[1,512,1024]{2,1,0:T(8,128)(2,1)S(1)} %fusion.36), channel_id=1, source_target_pairs={{0,1},{1,0},{2,3},{3,2},{4,5},{5,4},{6,7},{7,6},{8,9},{9,8},{10,11... | collective-permute-start | bytes 3145736 | tf_op jit(solution)/shard_map/ppermute | solution.py:140
  (23 other events, 242.1 us)
Sparse Core Ops, SparseCore 0:
  37.4 87.6 all-reduce.3
  128.3 44.2 all-gather.10
  174.9 40.2 all-gather.12
  218.0 49.3 all-gather.14
  270.3 49.0 all-gather.16
  394.9 52.3 all-gather.18
  451.5 60.5 reduce-scatter.6
  515.9 65.5 reduce-scatter.4
  585.4 72.0 reduce-scatter.8
  661.7 71.6 reduce-scatter.10

commit v2 on v1

--- a/solution.py
+++ b/solution.py
@@ -255,9 +255,8 @@
     placed = lax.dynamic_update_slice_in_dim(
         jnp.zeros((6 * width,), f32), mod_bias.astype(f32), owner * columns, 0
     )
-    modulation = lax.psum_scatter(
-        mod_term + placed, "fsdp", scatter_dimension=0, tiled=True
-    ).reshape(count, 6, 1, width)
+    terms = lax.all_to_all(mod_term + placed, "fsdp", split_axis=0, concat_axis=0, tiled=True)
+    modulation = jnp.sum(terms.reshape(fsdp, count, 6, 1, width), axis=0)
     shift_one = modulation[:, 0]
     scale_one = modulation[:, 1]
     gate_one = modulation[:, 2]
@@ -300,8 +299,8 @@
     rows = count * length
     flat_branch = grad_branch.reshape(rows, width)
     flat_pre = grad_pre.reshape(rows, -1)
-    down_part = scatter_rows(weight_term(hidden_act.reshape(rows, -1), flat_branch))
-    up_part = scatter_rows(weight_term(mlp_input.reshape(rows, width), flat_pre))
+    down_term = weight_term(hidden_act.reshape(rows, -1), flat_branch).astype(jnp.bfloat16)
+    up_term = weight_term(mlp_input.reshape(rows, width), flat_pre).astype(jnp.bfloat16)
     up_bias_term = jnp.sum(flat_pre.astype(f32), axis=0)
     own_branch = tokens.own(grad_branch)
     down_bias_term = jnp.sum(own_branch.astype(f32), axis=(0, 1))
@@ -317,7 +316,11 @@
     grad_attn = (gate_one * grad_after).astype(jnp.bfloat16)
     grad_gate_one = jnp.sum(grad_after * attn_out, axis=1)
     grad_heads = project_back(grad_attn, full_out).astype(jnp.bfloat16)
-    grad_mixed = tokens.to_heads(grad_heads)
+    grad_mixed, down_term, up_term = lax.optimization_barrier(
+        (tokens.to_heads(grad_heads), down_term, up_term)
+    )
+    down_part = scatter_rows(down_term)
+    up_part = scatter_rows(up_term)
     flat_attn = grad_attn.reshape(count * local_len, width)
     out_part = scatter_rows(weight_term(attn_heads.reshape(count * local_len, width), flat_attn))
     out_bias_term = jnp.sum(flat_attn.astype(f32), axis=0)
@@ -347,7 +350,7 @@
             up_bias_term,
         ]
     )
-    early = lax.all_gather(early, ("fsdp", "seq"), axis=0).reshape(fsdp, seq, -1)
+    early_size = early.shape[0]
     late = jnp.concatenate(
         [
             jnp.concatenate([grad_shift_one, grad_scale_one], axis=1).reshape(-1),
@@ -355,7 +358,10 @@
             column_sums[2 * part :],
         ]
     )
-    late = lax.all_gather(late, ("fsdp", "seq"), axis=0).reshape(fsdp, seq, -1)
+    both = lax.all_gather(
+        jnp.concatenate([early, late]), ("fsdp", "seq"), axis=0
+    ).reshape(fsdp, seq, -1)
+    early, late = both[:, :, :early_size], both[:, :, early_size:]
     at = count * 4 * width
     early_mod = jnp.sum(early[:, :, :at], axis=1).reshape(fsdp * count, 4 * width)
     early_bias = jnp.sum(early[:, :, at : at + 2 * width], axis=(0, 1))

time: 753 us -> 719 us (0.955)
  blocking collectives: 145 us -> 78.1 us
  waiting for transfers between devices: 341 us -> 385 us
  matrix products: 101 us -> 89 us
    reduce_scatter x4, waiting for transfers between devices: 68.9 us -> 194 us  [scatter_rows(): lax.psum_scatter(term.astype(jnp.bfloat16), 'fsdp', scatter_dimension=0,...]
    unnamed x11 -> x9, waiting for transfers between devices: 78.9 us -> 2.17 us
    all_gather x1 -> x0, blocking collectives: 68.3 us -> none  [per_device(): late = lax.all_gather(late, ('fsdp', 'seq'), axis=0).reshape(fsdp, seq, -1)]
    all_gather x4, waiting for transfers between devices: 93.5 us -> 47.6 us  [gather_rows(): return lax.all_gather(shard, 'fsdp', axis=0, tiled=True)]
    all_gather x1, waiting for transfers between devices: 0.01 us -> 43.8 us  [per_device(): lax.all_gather(jnp.concatenate([early, late]), ('fsdp', 'seq'), axis=0)]
    ppermute x8, waiting for transfers between devices: 100 us -> 83.9 us  [swap(): return lax.ppermute(values, 'seq', [(0, 1), (1, 0)])]
    all_to_all x0 -> x1, waiting for transfers between devices: none -> 14 us  [per_device(): lax.all_to_all(mod_term + placed, 'fsdp', split_axis=0, concat_axis=0, ti...]
  transfers between devices with their start and end apart: 18 -> 18, of which waited for: 13 -> 15; matrix products, arithmetic and copies ran while one was open for 15% -> 14% of each run, Pallas kernels for 11% -> 4%
where the time goes in v2:
time: 719 us; the launch traced here: 715 us
  waiting for transfers between devices  385 us (54%)
  matrix products  89 us (12%)
  Pallas kernels  81.7 us (11%)
  blocking collectives  78.1 us (11%)
  local copies, waits for them, and re-layouts  26.4 us (4%)
  other arithmetic  22.8 us (3%)
  starting transfers between devices  16.6 us (2%)
  between operations  14.8 us (2%)
    reduce_scatter x4, waiting for transfers between devices, scatter_rows(): lax.psum_scatter(term.astype(jnp.bfloat16), 'fsdp', scatter_dimension=0,...  194 us
    ppermute x8, waiting for transfers between devices, swap(): return lax.ppermute(values, 'seq', [(0, 1), (1, 0)])  83.9 us
    pallas_call x2, Pallas kernels, attend(): pl.pallas_call(functools.partial(kernel, block=block), grid=(count, part...  81.7 us
    all_gather x4, waiting for transfers between devices, gather_rows(): return lax.all_gather(shard, 'fsdp', axis=0, tiled=True)  47.6 us
    all_gather x1, waiting for transfers between devices, per_device(): lax.all_gather(jnp.concatenate([early, late]), ('fsdp', 'seq'), axis=0)  43.8 us
    dot_general x7, matrix products, project_back(): lax.dot_general(left, weight, (((left.ndim - 1,), (1,)), ((), ())), prefe...  30.9 us
    dot_general x5, matrix products, weight_term(): lax.dot_general(inputs, grads, (((0,), (0,)), ((), ())), preferred_elemen...  29.6 us
    dot_general x6, matrix products, project(): lax.dot_general(left, weight, (((left.ndim - 1,), (0,)), ((), ())), prefe...  28.4 us
  transfers between devices with their start and end apart: 18, of which 15 were waited for; matrix products, arithmetic and copies ran while one was open for 14% of the time, Pallas kernels for 4%

profile of v2, /device:TPU:0, one launch (start us, length us, event | category | flops | bytes accessed | tf_op | source)
XLA Modules:
  0.0 714.7 jit_solution(7437884416235602432)
XLA Ops:
  18.3 22.1 %all-gather.2 = bf16[16,1,1536]{2,1,0:T(2,128)(2,1)S(1)} all-gather(bf16[1,1,1536]{2,1,0:T(2,128)(2,1)S(1)} %reshape.600), channel_id=2, replica_groups=mesh['fsdp'=16,'seq'=2] {'fsdp'}, dimensions={0}, use_global_device_ids=true | all-gather | bytes 52224 | tf_op jit(solution)/shard_map/all_gather | solution.py:229
  48.2 14.0 %all-to-all-done = f32[16,1,6144]{2,1,0:T(1,128)S(1)} async-done(((f32[16,1,6144]{2,1,0:T(1,128)}), f32[16,1,6144]{2,1,0:T(1,128)S(1)}, u32[]{:S(2)}, u32[]{:S(2)}) %all-to-all-start) | async-done | bytes 393248 | tf_op jit(solution)/shard_map/all_to_all | solution.py:258
  72.6 30.2 %shard_map.245 = bf16[1,1024,512]{2,1,0:T(8,128)(2,1)S(1)} custom-call(bf16[1,1024,1536]{2,1,0:T(8,128)(2,1)S(1)} %fusion.10.query_ref.key_ref.value_ref, bf16[1,1024,1536]{2,1,0:T(8,128)(2,1)S(1)} %fusion.10.query_ref.key_ref.value_ref, bf16[1,1024,1536]{2,1,0:T(8,128)(2,1)S(1)} %fusion.10.query_ref.key_ref.value_ref), custom_call_target="tpu_custom_call" | custom-call | flops 8589934592 | bytes 4194304 | tf_op jit(solution)/shard_map/pallas_call | solution.py:118
  104.4 12.7 %collective-permute-done.1 = bf16[1,512,512]{2,1,0:T(8,128)(2,1)} collective-permute-done((bf16[1,512,512]{2,1,0:T(8,128)(2,1)S(1)}, bf16[1,512,512]{2,1,0:T(8,128)(2,1)}, u32[]{:S(2)}, u32[]{:S(2)}) %collective-permute-start.1) | collective-permute-done | bytes 524320 | tf_op jit(solution)/shard_map/ppermute | solution.py:140
  127.9 24.2 %collective-permute-done.2 = bf16[1,512,1024]{2,1,0:T(8,128)(2,1)} collective-permute-done((bf16[1,512,1024]{2,1,0:T(8,128)(2,1)}, bf16[1,512,1024]{2,1,0:T(8,128)(2,1)}, u32[]{:S(2)}, u32[]{:S(2)}) %collective-permute-start.2) | collective-permute-done | bytes 1048608 | tf_op jit(solution)/shard_map/ppermute | solution.py:140
  152.1 8.1 %all-gather.14.cloned.1.call-done = bf16[1024,2048]{1,0:T(8,128)(2,1)} async-done(((bf16[64,2048]{1,0:T(8,128)(2,1)}), bf16[1024,2048]{1,0:T(8,128)(2,1)}) %all-gather.14.cloned.1.call-update) | async-done | bytes 4194320 | tf_op jit(solution)/shard_map/all_gather | solution.py:184
  174.5 37.3 %all-gather.16.cloned.1.call-done = bf16[2048,1024]{1,0:T(8,128)(2,1)} async-done(((bf16[128,1024]{1,0:T(8,128)(2,1)}), bf16[2048,1024]{1,0:T(8,128)(2,1)}) %all-gather.16.cloned.1.call-update) | async-done | bytes 4194320 | tf_op jit(solution)/shard_map/all_gather | solution.py:184
  211.8 13.4 %convert_reduce_fusion = (f32[2048]{0:T(1024)S(1)}, bf16[1024,2048]{1,0:T(8,128)(2,1)S(1)}) fusion(f32[1024,2048]{1,0:T(8,128)} %copy-done.4, f32[2048]{0:T(1024)S(1)} %bitcast.179, bf16[2048,1024]{1,0:T(8,128)(2,1)} %all-gather.16.cloned.1.call-done, bf16[512,1024]{1,0:T(8,128)(2,1)} %bitcast.21, bf16[512,1024]{1,0:T(8,128)(2,1)} %bitcast.20, ...), kind=kOutput, calls=%fused_computation.9 | convolution fusion | flops 4349491200 | bytes 18894848 | tf_op jit(solution)/shard_map/dot_general | solution.py:35
  235.4 9.9 %convolution_convert_fusion.2 = bf16[2048,1024]{1,0:T(8,128)(2,1)} fusion(bf16[512,1024]{1,0:T(8,128)(2,1)} %bitcast.21, bf16[512,1024]{1,0:T(8,128)(2,1)} %bitcast.20, f32[1024]{0:T(1024)S(1)} %bitcast.192, f32[1024,2048]{1,0:T(8,128)S(1)} %bitcast.157, f32[2048]{0:T(1024)S(1)} %bitcast.180), kind=kOutput, calls=%fused_computation.23 | convolution fusion | flops 4324327424 | bytes 14692352 | tf_op jit(solution)/shard_map/dot_general | solution.py:41
  245.4 9.5 %collective-permute-done.5 = bf16[1,512,1024]{2,1,0:T(8,128)(2,1)} collective-permute-done((bf16[1,512,1024]{2,1,0:T(8,128)(2,1)}, bf16[1,512,1024]{2,1,0:T(8,128)(2,1)}, u32[]{:S(2)}, u32[]{:S(2)}) %collective-permute-start.5) | collective-permute-done | bytes 1048608 | tf_op jit(solution)/shard_map/ppermute | solution.py:140
  260.4 16.4 %collective-permute-done.3 = bf16[1,512,1024]{2,1,0:T(8,128)(2,1)} collective-permute-done((bf16[1,512,1024]{2,1,0:T(8,128)(2,1)}, bf16[1,512,1024]{2,1,0:T(8,128)(2,1)}, u32[]{:S(2)}, u32[]{:S(2)}) %collective-permute-start.3) | collective-permute-done | bytes 1048608 | tf_op jit(solution)/shard_map/ppermute | solution.py:140
  289.7 7.8 %convolution_convert_fusion.1 = bf16[1024,2048]{1,0:T(8,128)(2,1)} fusion(bf16[1024,2048]{1,0:T(8,128)(2,1)S(1)} %copy-done.33, bf16[1,512,1024]{2,1,0:T(8,128)(2,1)} %collective-permute-done.2, bf16[1,512,1024]{2,1,0:T(8,128)(2,1)} %add_convert_fusion.3), kind=kOutput, calls=%fused_computation.22 | convolution fusion | flops 4301258752 | bytes 10485760 | tf_op jit(solution)/shard_map/dot_general | solution.py:41
  301.5 51.4 %shard_map.246 = (bf16[1,1024,512]{2,1,0:T(8,128)(2,1)S(1)}, bf16[1,1024,512]{2,1,0:T(8,128)(2,1)S(1)}, bf16[1,1024,512]{2,1,0:T(8,128)(2,1)S(1)}) custom-call(bf16[1,1024,1536]{2,1,0:T(8,128)(2,1)} %copy-done.1, bf16[1,1024,1536]{2,1,0:T(8,128)(2,1)} %copy-done.1, bf16[1,1024,1536]{2,1,0:T(8,128)(2,1)} %copy-done.1, ...), custom_call_target="tpu_custom_call" | custom-call | flops 21474836480 | bytes 7340032 | tf_op jit(solution)/shard_map/pallas_call | solution.py:118
  364.5 17.0 %collective-permute-done.7 = bf16[1,512,1024]{2,1,0:T(8,128)(2,1)S(1)} collective-permute-done((bf16[1,512,1024]{2,1,0:T(8,128)(2,1)}, bf16[1,512,1024]{2,1,0:T(8,128)(2,1)S(1)}, u32[]{:S(2)}, u32[]{:S(2)}) %collective-permute-start.7) | collective-permute-done | bytes 1048608 | tf_op jit(solution)/shard_map/ppermute | solution.py:140
  397.5 23.7 %reduce-scatter.7.cloned.1.call-done = bf16[64,1024]{1,0:T(8,128)(2,1)} async-done(((bf16[1024,1024]{1,0:T(8,128)(2,1)}), bf16[64,1024]{1,0:T(8,128)(2,1)}) %reduce-scatter.7.cloned.1.call-update) | async-done | bytes 131088 | tf_op jit(solution)/shard_map/reduce_scatter | solution.py:188
  421.2 13.9 %all-reduce.1 = f32[64,1024]{1,0:T(8,128)} all-reduce(bf16[64,1024]{1,0:T(8,128)(2,1)} %reduce-scatter.7.cloned.1.call-done), channel_id=1, replica_groups=mesh['fsdp'=16,'seq'=2] {'seq'}, use_global_device_ids=true, to_apply=%region_27.28 | all-reduce | flops 65536 | bytes 393216 | tf_op jit(solution)/shard_map/psum | solution.py:409
  435.0 43.8 %all-gather.18.cloned.1.call-done = f32[360448]{0:T(1024)} async-done(((f32[11264]{0:T(1024)}), f32[360448]{0:T(1024)}) %all-gather.18.cloned.1.call-update) | async-done | bytes 1441808 | tf_op jit(solution)/shard_map/all_gather | solution.py:361
  482.1 20.4 %all-gather.3 = f32[16,64,16]{1,2,0:T(8,128)S(1)} all-gather(f32[1,64,16]{1,2,0:T(8,128)S(1)} %convolution_bitcast_fusion), channel_id=1, replica_groups=mesh['fsdp'=16,'seq'=2] {'fsdp'}, dimensions={0}, use_global_device_ids=true | all-gather | bytes 69632 | tf_op jit(solution)/shard_map/all_gather | solution.py:393
  509.4 38.9 %reduce-scatter.5.cloned.1.call-done = bf16[64,1536]{1,0:T(8,128)(2,1)} async-done(((bf16[1024,1536]{1,0:T(8,128)(2,1)}), bf16[64,1536]{1,0:T(8,128)(2,1)}) %reduce-scatter.5.cloned.1.call-update) | async-done | bytes 196624 | tf_op jit(solution)/shard_map/reduce_scatter | solution.py:188
  549.3 7.5 %all_gather.45 = bf16[64,3,1024]{2,1,0:T(4,128)(2,1)S(1)} all-gather(bf16[64,3,512]{2,1,0:T(4,128)(2,1)S(1)} %reshape.585), channel_id=1, replica_groups=mesh['fsdp'=16,'seq'=2] {'seq'}, dimensions={2}, use_global_device_ids=true | all-gather | bytes 589824 | tf_op jit(solution)/shard_map/all_gather | solution.py:405
  557.9 66.5 %reduce-scatter.9.cloned.1.call-done = bf16[64,2048]{1,0:T(8,128)(2,1)} async-done(((bf16[1024,2048]{1,0:T(8,128)(2,1)}), bf16[64,2048]{1,0:T(8,128)(2,1)}) %reduce-scatter.9.cloned.1.call-update) | async-done | bytes 262160 | tf_op jit(solution)/shard_map/reduce_scatter | solution.py:188
  625.4 7.0 all_gather.46
  634.8 64.9 %reduce-scatter.11.cloned.1.call-done = bf16[128,1024]{1,0:T(8,128)(2,1)} async-done(((bf16[2048,1024]{1,0:T(8,128)(2,1)}), bf16[128,1024]{1,0:T(8,128)(2,1)}) %reduce-scatter.11.cloned.1.call-update) | async-done | bytes 262160 | tf_op jit(solution)/shard_map/reduce_scatter | solution.py:188
  699.6 7.2 %all_gather.47 = bf16[256,1024]{1,0:T(8,128)(2,1)S(1)} all-gather(bf16[128,1024]{1,0:T(8,128)(2,1)} %reduce-scatter.11.cloned.1.call-done), channel_id=1, replica_groups=mesh['fsdp'=16,'seq'=2] {'seq'}, dimensions={0}, use_global_device_ids=true | all-gather | bytes 786432 | tf_op jit(solution)/shard_map/all_gather | solution.py:398
  (208 shorter events, 132.2 us)
Async XLA Ops:
  7.2 33.4 %copy-start = (bf16[64,6144]{1,0:T(8,128)(2,1)S(1)}, bf16[64,6144]{1,0:T(8,128)(2,1)}, u32[]{:S(2)}) copy-start(bf16[64,6144]{1,0:T(8,128)(2,1)} %param.16) | copy-start | bytes 2359300
  7.3 33.1 %copy-start.21 = (bf16[384]{0:T(512)(128)(2,1)S(1)}, bf16[384]{0:T(512)(128)(2,1)}, u32[]{:S(2)}) copy-start(bf16[384]{0:T(512)(128)(2,1)} %param.17) | copy-start | bytes 2308
  7.3 58.5 %all-gather.10.cloned.1.call-start = ((), (), s32[]{:S(2)}) async-start(), calls=%async_computation.5 | async-start | bytes 3342336 | tf_op jit(solution)/shard_map/all_gather | solution.py:184
  10.0 109.1 %all-gather.12.cloned.1.call-start = ((), (), s32[]{:S(2)}) async-start(), calls=%async_computation.6 | async-start | bytes 2228224 | tf_op jit(solution)/shard_map/all_gather | solution.py:184
  10.7 149.4 %all-gather.14.cloned.1.call-start = ((), (), s32[]{:S(2)}) async-start(), calls=%async_computation.7 | async-start | bytes 4456448 | tf_op jit(solution)/shard_map/all_gather | solution.py:184
  14.5 48.0 %collective-permute-start = (bf16[1,512,1024]{2,1,0:T(8,128)(2,1)S(1)}, bf16[1,512,1024]{2,1,0:T(8,128)(2,1)S(1)}, u32[]{:S(2)}, u32[]{:S(2)}) collective-permute-start(bf16[1,512,1024]{2,1,0:T(8,128)(2,1)S(1)} %copy-done.2), channel_id=1, source_target_pairs={{0,1},{1,0},{2,3},{3,2},{4,5},{5,4},{6,7},{7,6},{8,9},{9,8},{10,11... | collective-permute-start | bytes 3145736 | tf_op jit(solution)/shard_map/ppermute | solution.py:140
  42.0 20.2 %all-to-all-start = ((f32[16,1,6144]{2,1,0:T(1,128)}), f32[16,1,6144]{2,1,0:T(1,128)S(1)}, u32[]{:S(2)}, u32[]{:S(2)}) async-start(f32[16,1,6144]{2,1,0:T(1,128)} %copy.43), calls=%async_computation | async-start | bytes 786432 | tf_op jit(solution)/shard_map/all_to_all | solution.py:258
  45.6 166.2 %all-gather.16.cloned.1.call-start = ((), (), s32[]{:S(2)}) async-start(), calls=%async_computation.8 | async-start | bytes 4456448 | tf_op jit(solution)/shard_map/all_gather | solution.py:184
  47.3 373.8 %reduce-scatter.7.cloned.1.call-start = ((), (), s32[]{:S(2)}) async-start(), calls=%async_computation.10 | async-start | bytes 2228224 | tf_op jit(solution)/shard_map/reduce_scatter | solution.py:188
  72.6 30.3 %copy-start.1 = (bf16[1,1024,1536]{2,1,0:T(8,128)(2,1)}, bf16[1,1024,1536]{2,1,0:T(8,128)(2,1)S(1)}, u32[]{:S(2)}) copy-start(bf16[1,1024,1536]{2,1,0:T(8,128)(2,1)S(1)} %fusion.10.query_ref.key_ref.value_ref) | copy-start | bytes 9437188
  102.9 14.2 %collective-permute-start.1 = (bf16[1,512,512]{2,1,0:T(8,128)(2,1)S(1)}, bf16[1,512,512]{2,1,0:T(8,128)(2,1)}, u32[]{:S(2)}, u32[]{:S(2)}) collective-permute-start(bf16[1,512,512]{2,1,0:T(8,128)(2,1)S(1)} %slice.150), channel_id=1, source_target_pairs={{0,1},{1,0},{2,3},{3,2},{4,5},{5,4},{6,7},{7,6},{8,9},{9,8},{10,11... | collective-permute-start | bytes 1572872 | tf_op jit(solution)/shard_map/ppermute | solution.py:140
  125.6 26.4 %collective-permute-start.2 = (bf16[1,512,1024]{2,1,0:T(8,128)(2,1)}, bf16[1,512,1024]{2,1,0:T(8,128)(2,1)}, u32[]{:S(2)}, u32[]{:S(2)}) collective-permute-start(bf16[1,512,1024]{2,1,0:T(8,128)(2,1)} %add_convert_fusion.3), channel_id=1, source_target_pairs={{0,1},{1,0},{2,3},{3,2},{4,5},{5,4},{6,7},{7,6},{8,9},{9,8},{10,11... | collective-permute-start | bytes 3145736 | tf_op jit(solution)/shard_map/ppermute | solution.py:140
  126.8 47.7 %collective-permute-start.4 = (bf16[1,512,1024]{2,1,0:T(8,128)(2,1)}, bf16[1,512,1024]{2,1,0:T(8,128)(2,1)}, u32[]{:S(2)}, u32[]{:S(2)}) collective-permute-start(bf16[1,512,1024]{2,1,0:T(8,128)(2,1)} %param.27), channel_id=1, source_target_pairs={{0,1},{1,0},{2,3},{3,2},{4,5},{5,4},{6,7},{7,6},{8,9},{9,8},{10,11... | collective-permute-start | bytes 3145736 | tf_op jit(solution)/shard_map/ppermute | solution.py:140
  228.6 26.3 %collective-permute-start.5 = (bf16[1,512,1024]{2,1,0:T(8,128)(2,1)}, bf16[1,512,1024]{2,1,0:T(8,128)(2,1)}, u32[]{:S(2)}, u32[]{:S(2)}) collective-permute-start(bf16[1,512,1024]{2,1,0:T(8,128)(2,1)} %fusion.34), channel_id=1, source_target_pairs={{0,1},{1,0},{2,3},{3,2},{4,5},{5,4},{6,7},{7,6},{8,9},{9,8},{10,11... | collective-permute-start | bytes 3145736 | tf_op jit(solution)/shard_map/ppermute | solution.py:140
  233.9 42.8 %collective-permute-start.3 = (bf16[1,512,1024]{2,1,0:T(8,128)(2,1)}, bf16[1,512,1024]{2,1,0:T(8,128)(2,1)}, u32[]{:S(2)}, u32[]{:S(2)}) collective-permute-start(bf16[1,512,1024]{2,1,0:T(8,128)(2,1)} %fusion.35), channel_id=1, source_target_pairs={{0,1},{1,0},{2,3},{3,2},{4,5},{5,4},{6,7},{7,6},{8,9},{9,8},{10,11... | collective-permute-start | bytes 3145736 | tf_op jit(solution)/shard_map/ppermute | solution.py:140
  245.3 31.4 %copy-start.11 = (bf16[1,1024,2048]{2,1,0:T(8,128)(2,1)S(1)}, bf16[1,1024,2048]{2,1,0:T(8,128)(2,1)}, u32[]{:S(2)}) copy-start(bf16[1,1024,2048]{2,1,0:T(8,128)(2,1)} %fusion.58) | copy-start | bytes 12582916
  245.4 31.4 %copy-start.29 = (bf16[2048,1024]{1,0:T(8,128)(2,1)S(1)}, bf16[2048,1024]{1,0:T(8,128)(2,1)}, u32[]{:S(2)}) copy-start(bf16[2048,1024]{1,0:T(8,128)(2,1)} %all-gather.16.cloned.1.call-done) | copy-start | bytes 12582916
  288.1 13.3 %collective-permute-start.6 = (bf16[1,512,512]{2,1,0:T(8,128)(2,1)S(1)}, bf16[1,512,512]{2,1,0:T(8,128)(2,1)S(1)}, u32[]{:S(2)}, u32[]{:S(2)}) collective-permute-start(bf16[1,512,512]{2,1,0:T(8,128)(2,1)S(1)} %get-tuple-element.57), channel_id=1, source_target_pairs={{0,1},{1,0},{2,3},{3,2},{4,5},{5,4},{6,7},{7,6},{8,9},{9,8},{10,11... | collective-permute-start | bytes 1572872 | tf_op jit(solution)/shard_map/ppermute | solution.py:140
  357.7 23.8 %collective-permute-start.7 = (bf16[1,512,1024]{2,1,0:T(8,128)(2,1)}, bf16[1,512,1024]{2,1,0:T(8,128)(2,1)S(1)}, u32[]{:S(2)}, u32[]{:S(2)}) collective-permute-start(bf16[1,512,1024]{2,1,0:T(8,128)(2,1)} %fusion.37), channel_id=1, source_target_pairs={{0,1},{1,0},{2,3},{3,2},{4,5},{5,4},{6,7},{7,6},{8,9},{9,8},{10,11... | collective-permute-start | bytes 3145736 | tf_op jit(solution)/shard_map/ppermute | solution.py:140
  361.9 116.9 %all-gather.18.cloned.1.call-start = ((), (), s32[]{:S(2)}) async-start(), calls=%async_computation.13 | async-start | bytes 1486848 | tf_op jit(solution)/shard_map/all_gather | solution.py:361
  388.9 159.4 %reduce-scatter.5.cloned.1.call-start = ((), (), s32[]{:S(2)}) async-start(), calls=%async_computation.9 | async-start | bytes 3342336 | tf_op jit(solution)/shard_map/reduce_scatter | solution.py:188
  396.0 228.4 %reduce-scatter.9.cloned.1.call-start = ((), (), s32[]{:S(2)}) async-start(), calls=%async_computation.11 | async-start | bytes 4456448 | tf_op jit(solution)/shard_map/reduce_scatter | solution.py:188
  396.8 302.9 %reduce-scatter.11.cloned.1.call-start = ((), (), s32[]{:S(2)}) async-start(), calls=%async_computation.12 | async-start | bytes 4456448 | tf_op jit(solution)/shard_map/reduce_scatter | solution.py:188
  480.9 27.8 %copy-start.19 = (bf16[1,1024]{1,0:T(2,128)(2,1)S(1)}, bf16[1,1024]{1,0:T(2,128)(2,1)}, u32[]{:S(2)}) copy-start(bf16[1,1024]{1,0:T(2,128)(2,1)} %param.15) | copy-start | bytes 6148
  (30 other events, 260.7 us)
Sparse Core Ops, SparseCore 0:
  11.0 54.7 all-gather.9
  68.0 40.0 all-gather.11
  110.7 49.3 all-gather.13
  162.7 49.0 all-gather.15
  362.0 59.1 reduce-scatter.6
  424.9 53.8 all-gather.17
  483.1 65.1 reduce-scatter.4
  552.6 71.7 reduce-scatter.8
  628.2 71.3 reduce-scatter.10
